TPU v7x, 128 devices: a whole 4x4x4 slice. The times are simulated.
128 devices in a mesh: crow: 16 (over z, x), ccol: 8 (over y, core).
Axes of the slice: x: 4, y: 4, z: 4, core: 2. Of those that a mesh axis runs over, the one named last changes fastest.
Arguments:
- sketch: float32 [524288, 512], P(('crow', 'ccol')), may hold values from -120 to 120, as said below
Outputs:
- posterior_basis: float32 [524288, 512], P(('crow', 'ccol'))
- mean_log_eigen: float32 [], replicated
Inputs may be any that keep to these rules, and one draw needn't show every extreme that they name: Entries of the sketch are real numbers of either sign.
All inputs are finite; a program needn't handle non-finite values.
Results may differ from a plain program's by a relative error of at most 0.0003.
Values sent between devices are 32-bit elements; how exact they have to be, the bound alone decides.
A program may use at most 128 MiB of HBM per device.

v0:
```python
import math

import jax
import jax.numpy as jnp
from jax import lax
from jax.sharding import PartitionSpec as P


def on_device(sketch):
    rows_dev = sketch.shape[0]
    width = sketch.shape[1]
    rows_all = rows_dev * lax.axis_size("crow") * lax.axis_size("ccol")
    eye = jnp.eye(width, dtype=jnp.float32)
    partial_value = lax.dot_general(
        sketch,
        sketch,
        (((0,), (0,)), ((), ())),
        precision=lax.Precision.HIGHEST,
        preferred_element_type=jnp.float32,
    )
    summed = lax.psum(partial_value, ("crow", "ccol"))
    summed = summed + jnp.float32(rows_all) * eye
    factor = jnp.linalg.cholesky(summed)
    inverse = jax.scipy.linalg.cho_solve((factor, True), jnp.float32(rows_all) * eye)
    inverse = 0.5 * (inverse + inverse.T)
    posterior_basis = jnp.dot(
        sketch, inverse, precision=lax.Precision.HIGHEST, preferred_element_type=jnp.float32
    )
    logdet = 2.0 * jnp.sum(jnp.log(jnp.diagonal(factor))) - width * math.log(rows_all)
    return (posterior_basis, logdet / jnp.float32(width))


def solution(mesh):
    return jax.shard_map(
        on_device,
        mesh=mesh,
        in_specs=(P(("crow", "ccol"), None),),
        out_specs=(P(("crow", "ccol"), None), P()),
        check_vma=False,
    )
```

profile of v0, /device:TPU:1, one launch (start us, length us, event | category | flops | bytes accessed | tf_op | source)
XLA Modules:
  0.0 383.4 jit_solution(1382514454104315068)
XLA Ops:
  7.2 18.8 %fusion.55 = f32[512,512]{0,1:T(8,128)} fusion(f32[4096,512]{1,0:T(8,128)} %param.1), kind=kOutput, calls=%fused_computation.99 | convolution fusion | flops 12884901888 | bytes 9437184 | tf_op jit(solution)/shard_map/dot_general | solution.py:14
  26.1 1.1 fusion.4
  27.2 149.6 %all-reduce.3.cloned.1.call-done = f32[512,512]{0,1:T(8,128)} async-done(((f32[512,512]{0,1:T(8,128)}), f32[512,512]{0,1:T(8,128)}) %all-reduce.3.cloned.1.call-update) | async-done | bytes 1048592 | tf_op jit(solution)/shard_map/psum | solution.py:21
  176.8 1.3 fusion.22
  178.4 1.5 fusion.2
  179.9 11.7 %cholesky.103 = f32[128,128]{1,0:T(8,128)S(1)} custom-call(f32[128,128]{1,0:T(8,128)S(1)} %cholesky.263), custom_call_target="Cholesky" | custom-call | tf_op jit(solution)/shard_map/jit(cholesky)/cholesky | solution.py:23
  191.8 9.8 %custom-call.34 = f32[1,128,128]{1,2,0:T(8,128)S(1)} custom-call(f32[1,128,128]{2,1,0:T(8,128)S(1)} %get-tuple-element.39), custom_call_target="InvertDiagBlocksLowerTriangular" | custom-call | tf_op jit(solution)/shard_map/jit(cholesky)/cholesky | solution.py:23
  202.4 11.7 %cholesky.215 = f32[128,128]{1,0:T(8,128)S(1)} custom-call(f32[128,128]{1,0:T(8,128)S(1)} %cholesky.267), custom_call_target="Cholesky" | custom-call | tf_op jit(solution)/shard_map/jit(cholesky)/cholesky | solution.py:23
  214.3 10.0 %custom-call.35 = f32[1,128,128]{1,2,0:T(8,128)S(1)} custom-call(f32[1,128,128]{2,1,0:T(8,128)S(1)} %get-tuple-element.37), custom_call_target="InvertDiagBlocksLowerTriangular" | custom-call | tf_op jit(solution)/shard_map/jit(cholesky)/cholesky | solution.py:23
  225.3 11.7 %cholesky.236 = f32[128,128]{1,0:T(8,128)S(1)} custom-call(f32[128,128]{1,0:T(8,128)S(1)} %cholesky.272), custom_call_target="Cholesky" | custom-call | tf_op jit(solution)/shard_map/jit(cholesky)/cholesky | solution.py:23
  237.2 9.8 %custom-call.36 = f32[1,128,128]{1,2,0:T(8,128)S(1)} custom-call(f32[1,128,128]{2,1,0:T(8,128)S(1)} %get-tuple-element.35), custom_call_target="InvertDiagBlocksLowerTriangular" | custom-call | tf_op jit(solution)/shard_map/jit(cholesky)/cholesky | solution.py:23
  247.8 11.9 %cholesky.253 = f32[128,128]{1,0:T(8,128)S(1)} custom-call(f32[128,128]{1,0:T(8,128)S(1)} %convolution_subtract_fusion.8), custom_call_target="Cholesky" | custom-call | tf_op jit(solution)/shard_map/jit(cholesky)/cholesky | solution.py:23
  259.8 0.7 compare_reduce_fusion.1
  260.6 0.6 compare_reduce_fusion
  261.2 0.7 compare_reduce_fusion.2
  264.7 11.0 %while.1 = (s32[]{:T(128)}, f32[512,512]{0,1:T(8,128)S(1)}, s32[4,2]{0,1:T(2,128)S(1)}, f32[4,128,128]{2,1,0:T(8,128)}, s32[]{:T(128)}) while((s32[]{:T(128)}, f32[512,512]{0,1:T(8,128)S(1)}, s32[4,2]{0,1:T(2,128)S(1)}, f32[4,128,128]{2,1,0:T(8,128)}, s32[]{:T(128)}) %tuple.32), condition=%wide.while_cond, body=%wide.while_body.sunk | while | flops 2 | bytes 393329 | solution.py:24
  265.4 1.3 dynamic-slice.7
  266.8 0.6 bitcast_dynamic-update-slice_fusion.2
  268.1 1.3 dynamic-slice.7
  270.9 1.3 dynamic-slice.7
  273.6 1.3 dynamic-slice.7
  275.0 0.6 bitcast_dynamic-update-slice_fusion.2
  275.7 40.1 %custom-call.37 = f32[4,128,128]{1,2,0:T(8,128)S(1)} custom-call(f32[4,128,128]{2,1,0:T(8,128)} %get-tuple-element.9), custom_call_target="InvertDiagBlocksLowerTriangular" | custom-call | tf_op jit(solution)/shard_map/jit(_cho_solve)/triangular_solve | solution.py:24
  315.8 1.4 fusion.23
  317.2 1.5 convolution_subtract_fusion.3
  319.1 2.0 convolution_subtract_fusion.2
  321.5 2.4 convolution_subtract_fusion.5
  326.3 1.3 convolution_subtract_fusion.4
  328.1 4.5 %gather_fusion = f32[512]{0:T(512)S(1)} fusion(f32[512,512]{0,1:T(8,128)S(1)} %get-tuple-element.31, s32[512]{0:T(512)S(1)} %bitcast.66), kind=kCustom, calls=%fused_computation | custom fusion | bytes 8192 | tf_op jit(solution)/shard_map/jit(diagonal)/cond/branch_0_fun/gather | solution.py:29
  333.2 1.5 fusion.42
  335.2 30.3 %convolution_bitcast_fusion = f32[4096,512]{0,1:T(8,128)} fusion(f32[4096,512]{1,0:T(8,128)} %param.1, f32[512,512]{1,0:T(8,128)S(1)} %copy.33, f32[128,512]{0,1:T(8,128)S(1)} %copy.32, f32[128,512]{0,1:T(8,128)S(1)} %copy.31, f32[128,512]{0,1:T(8,128)S(1)} %copy.30, f32[128,512]{0,1:T(8,128)S(1)} %fusion.42), kind=kOutput, calls=%fused_computation.3 | convolution fusion | flops 12886212608 | bytes 18874368 | tf_op jit(solution)/shard_map/dot_general | solution.py:26
  365.5 8.9 %copy.34 = f32[4096,512]{1,0:T(8,128)} copy(f32[4096,512]{0,1:T(8,128)} %convolution_bitcast_fusion) | data formatting | bytes 16777216
  (59 shorter events, 12.7 us)
Async XLA Ops:
  7.2 169.6 %all-reduce.3.cloned.1.call-start = ((), (), s32[]{:S(2)}) async-start(), calls=%async_computation | async-start | bytes 2097152 | tf_op jit(solution)/shard_map/psum | solution.py:21
Sparse Core Ops, SparseCore 0:
  26.2 150.5 all-reduce.2
where the time goes:
time: 387 us; the launch traced here: 383 us
  waiting for transfers between devices  150 us (39%)
  other arithmetic  124 us (32%)
  matrix products  64.8 us (17%)
  local copies, waits for them, and re-layouts  26.1 us (7%)
  between operations  19 us (5%)
    psum x1, waiting for transfers between devices, on_device(): summed = lax.psum(partial_value, ('crow', 'ccol'))  150 us
    another operation x14, other arithmetic, on_device(): factor = jnp.linalg.cholesky(summed)  78.8 us
    another operation x4, other arithmetic, on_device(): jax.scipy.linalg.cho_solve((factor, True), jnp.float32(rows_all) * eye)  40.4 us
    dot_general x1, matrix products, on_device(): jnp.dot(sketch, inverse, precision=lax.Precision.HIGHEST, preferred_eleme...  30.3 us
    dot_general x1, matrix products, on_device(): lax.dot_general(sketch, sketch, (((0,), (0,)), ((), ())), precision=lax.P...  18.8 us
    another operation x14, matrix products, on_device(): jax.scipy.linalg.cho_solve((factor, True), jnp.float32(rows_all) * eye)  13.3 us
    another operation x20, local copies, waits for them, and re-layouts  10.9 us
    unnamed x1, local copies, waits for them, and re-layouts  8.94 us
  transfers between devices with their start and end apart: 1, of which 1 were waited for; matrix products, arithmetic and copies ran while one was open for 0% of the time, Pallas kernels for 0%

commit v1 on v0

v1 whole, which is shorter than its diff:
```python
import functools

import jax
import jax.numpy as jnp
from jax import lax
from jax.experimental import pallas as pl
from jax.experimental.pallas import tpu as pltpu
from jax.sharding import PartitionSpec as P

MESH = pl.DeviceIdType.MESH
F32, BF16 = jnp.float32, jnp.bfloat16
VMEM_LIMIT = 60 * 2**20
CHUNK = 512
GROUP = 16


def split(x):
    high = x.astype(BF16)
    return high, (x - high.astype(F32)).astype(BF16)


def place():
    crow, ccol = lax.axis_index("crow"), lax.axis_index("ccol")
    return crow // 4, crow % 4, ccol // 2, ccol % 2


def peer(here, offset):
    z, x, y, core = here
    dz, dx, dy = offset
    return (((z + dz) % 4) * 4 + (x + dx) % 4, ((y + dy) % 4) * 2 + core)


def hops(offset):
    return sum(min(d, 4 - d) for d in offset)


OFFSETS = sorted(
    [(dz, dx, dy) for dz in range(4) for dx in range(4) for dy in range(4) if (dz, dx, dy) != (0, 0, 0)],
    key=lambda o: (-hops(o), o),
)


def gram_kernel(x_hbm, out, xb, acc, cross, part, crecv, mine, rbuf, load_sem, core_sem, rs_sem, ag_sem, fw_sem):
    rows = x_hbm.shape[0]
    n = rows // CHUNK
    loads = [
        pltpu.make_async_copy(x_hbm.at[pl.ds(i * CHUNK, CHUNK)], xb.at[pl.ds(i * CHUNK, CHUNK)], load_sem.at[i])
        for i in range(n)
    ]
    for load in loads:
        load.start()

    here = place()
    z, x, y, core = here
    chip = (z * 4 + x) * 4 + y
    crow, ccol = lax.axis_index("crow"), lax.axis_index("ccol")
    twin = (crow, ccol + 1 - 2 * core)
    barrier = pltpu.get_barrier_semaphore()
    pl.semaphore_signal(barrier, inc=1, device_id=twin, device_id_type=MESH)
    for offset in OFFSETS:
        pl.semaphore_signal(barrier, inc=1, device_id=peer(here, offset), device_id_type=MESH)

    dims = (((0,), (0,)), ((), ()))
    for i in range(n):
        loads[i].wait()
        high, low = split(xb[i * CHUNK : (i + 1) * CHUNK, :])
        a = lax.dot_general(high, high, dims, preferred_element_type=F32)
        b = lax.dot_general(high, low, dims, preferred_element_type=F32)
        if i == 0:
            acc[...] = a
            cross[...] = b
        else:
            acc[...] += a
            cross[...] += b
    b = cross[...]
    total = acc[...] + b + b.T
    width = total.shape[1] // 2
    for half in range(2):
        part[half] = total[:, half * width : (half + 1) * width].reshape(64, 8, width)

    pl.semaphore_wait(barrier, 1 + len(OFFSETS))
    swap = pltpu.make_async_remote_copy(
        src_ref=part.at[1 - core],
        dst_ref=crecv,
        send_sem=core_sem.at[0],
        recv_sem=core_sem.at[1],
        device_id=twin,
        device_id_type=MESH,
    )
    swap.start()
    swap.wait()
    mine[...] = part[core] + crecv[...]

    def scatter(s, offset):
        dz, dx, dy = offset
        target = (((z + dz) % 4) * 4 + (x + dx) % 4) * 4 + (y + dy) % 4
        return pltpu.make_async_remote_copy(
            src_ref=mine.at[target],
            dst_ref=rbuf.at[s],
            send_sem=rs_sem.at[0],
            recv_sem=rs_sem.at[1],
            device_id=peer(here, offset),
            device_id_type=MESH,
        )

    for s, offset in enumerate(OFFSETS):
        scatter(s, offset).start()
    pltpu.make_async_copy(rbuf, rbuf, rs_sem.at[1]).wait()
    sums = [mine[chip]] + [rbuf[s] for s in range(63)]
    while len(sums) > 1:
        sums = [a + b for a, b in zip(sums[0::2], sums[1::2])]
    out[core, chip] = sums[0]
    for s, offset in enumerate(OFFSETS):
        pltpu.make_async_remote_copy(
            src_ref=out.at[core, chip],
            dst_ref=out.at[core, chip],
            send_sem=ag_sem.at[0],
            recv_sem=ag_sem.at[1],
            device_id=peer(here, offset),
            device_id_type=MESH,
        ).start()
    pltpu.make_async_copy(rbuf, rbuf, ag_sem.at[1]).wait()
    forward = pltpu.make_async_remote_copy(
        src_ref=out.at[core],
        dst_ref=out.at[core],
        send_sem=fw_sem.at[0],
        recv_sem=fw_sem.at[1],
        device_id=twin,
        device_id_type=MESH,
    )
    forward.start()
    pltpu.make_async_copy(rbuf, rbuf, rs_sem.at[0]).wait()
    pltpu.make_async_copy(rbuf, rbuf, ag_sem.at[0]).wait()
    forward.wait()


def sub_row(x, s):
    return jnp.broadcast_to(x[s : s + 1, :], (8, 128))


def lane_col(x, j):
    return jnp.broadcast_to(x[:, j : j + 1], (8, 128))


def invert_leaf(rows):
    lane = lax.broadcasted_iota(jnp.int32, (8, 128), 1)
    sub = lax.broadcasted_iota(jnp.int32, (8, 128), 0)
    rows = list(rows)
    pivots = jnp.ones((8, 128), F32)
    nv = GROUP // 8
    for g in range(128 // GROUP):
        a = GROUP * g
        own = [nv * g + v for v in range(nv)]
        others = [i for i in range(16) if i > own[-1]] + [i for i in range(16) if i < own[0]]
        cols = [[lane_col(rows[m], a + j) for m in own] for j in range(GROUP)]
        left = {i: [lane_col(rows[i], a + j) for j in range(GROUP)] for i in others}
        inside = (lane >= a) & (lane < a + GROUP)
        top = [jnp.where(inside, (lane - a == sub + 8 * v).astype(F32), rows[m]) for v, m in enumerate(own)]
        scale = [None] * nv
        for k in range(GROUP):
            kv, ks = divmod(k, 8)
            pivot = sub_row(cols[k][kv], ks)
            r = 1.0 / pivot
            pivots = jnp.where(lane == a + k, pivot, pivots)
            scale[kv] = r if scale[kv] is None else jnp.where(sub == ks, r, scale[kv])
            rest = [jnp.where(sub == ks, 0.0, cols[k][v]) if v == kv else cols[k][v] for v in range(nv)]
            factor = [rest[v] * r for v in range(nv)]
            for j in range(k + 1, GROUP):
                b = sub_row(cols[j][kv], ks)
                if j == k + 1:
                    cols[j] = [cols[j][v] - (rest[v] * b) * r for v in range(nv)]
                else:
                    cols[j] = [cols[j][v] - factor[v] * b for v in range(nv)]
            b = sub_row(top[kv], ks)
            top = [top[v] - factor[v] * b for v in range(nv)]
        top = [top[v] * scale[v] for v in range(nv)]
        for v, m in enumerate(own):
            rows[m] = top[v]
        spread = [sub_row(top[j // 8], j % 8) for j in range(GROUP)]
        for i in others:
            value = jnp.where(inside, 0.0, rows[i])
            for j in range(GROUP):
                value = value - left[i][j] * spread[j]
            rows[i] = value
    return rows, pivots


def dot_exact(a, b):
    return jnp.dot(a, b, precision=lax.Precision.HIGHEST, preferred_element_type=F32)


def map_kernel(total, gram, x_hbm, out_hbm, logdet, xb, ob, mat, load_sem, store_sem):
    rows, k = x_hbm.shape
    n = rows // CHUNK
    loads = [
        pltpu.make_async_copy(x_hbm.at[pl.ds(i * CHUNK, CHUNK)], xb.at[pl.ds(i * CHUNK, CHUNK)], load_sem.at[i])
        for i in range(n)
    ]
    for load in loads:
        load.start()
    half = k // 2
    eye = (lax.broadcasted_iota(jnp.int32, (k, k), 0) == lax.broadcasted_iota(jnp.int32, (k, k), 1)).astype(F32)
    mat[...] = eye
    for c in range(2):
        mat[:, c * half : (c + 1) * half] += gram[c].reshape(k, half) * (1.0 / total)

    logs = jnp.zeros((8, 128), F32)
    unit = eye[:128, :128]
    for b in range(k // 128):
        lo, hi = 128 * b, 128 * (b + 1)
        leaf, pivots = invert_leaf([mat[lo + 8 * i : lo + 8 * i + 8, lo:hi] for i in range(16)])
        logs = logs + jnp.log(pivots)
        inverse = jnp.concatenate(leaf, axis=0)
        mat[lo:hi, lo:hi] = unit
        top = dot_exact(inverse, mat[lo:hi, :])
        for i in range(k // 128):
            if i != b:
                side = mat[128 * i : 128 * i + 128, lo:hi]
                mat[128 * i : 128 * i + 128, lo:hi] = jnp.zeros((128, 128), F32)
                mat[128 * i : 128 * i + 128, :] -= dot_exact(side, top)
        mat[lo:hi, :] = top
    logdet[...] = jnp.broadcast_to(jnp.sum(logs[0:1, :], axis=1, keepdims=True), (8, 128)) * (1.0 / k)

    high, low = split(mat[...])
    stores = []
    for i in range(n):
        loads[i].wait()
        xh, xl = split(xb[i * CHUNK : (i + 1) * CHUNK, :])
        y = jnp.dot(xl, high, preferred_element_type=F32) + jnp.dot(xh, low, preferred_element_type=F32)
        ob[i * CHUNK : (i + 1) * CHUNK, :] = jnp.dot(xh, high, preferred_element_type=F32) + y
        store = pltpu.make_async_copy(
            ob.at[pl.ds(i * CHUNK, CHUNK)], out_hbm.at[pl.ds(i * CHUNK, CHUNK)], store_sem.at[i]
        )
        store.start()
        stores.append(store)
    for store in stores:
        store.wait()


def on_device(sketch):
    rows, k = sketch.shape
    total = rows * lax.axis_size("crow") * lax.axis_size("ccol")
    n = rows // CHUNK
    half = k // 2
    vmem, anywhere = pl.BlockSpec(memory_space=pltpu.VMEM), pl.BlockSpec(memory_space=pl.ANY)
    dma = pltpu.SemaphoreType.DMA
    gram = pl.pallas_call(
        gram_kernel,
        out_shape=jax.ShapeDtypeStruct((2, 64, 8, half), F32),
        in_specs=[anywhere],
        out_specs=vmem,
        scratch_shapes=[
            pltpu.VMEM((rows, k), F32),
            pltpu.VMEM((k, k), F32),
            pltpu.VMEM((k, k), F32),
            pltpu.VMEM((2, 64, 8, half), F32),
            pltpu.VMEM((64, 8, half), F32),
            pltpu.VMEM((64, 8, half), F32),
            pltpu.VMEM((63, 8, half), F32),
            dma((n,)),
            dma((2,)),
            dma((2,)),
            dma((2,)),
            dma((2,)),
        ],
        compiler_params=pltpu.CompilerParams(
            collective_id=0, has_side_effects=True, vmem_limit_bytes=VMEM_LIMIT
        ),
        name="gram_sum",
    )(sketch)
    basis, logdet = pl.pallas_call(
        functools.partial(map_kernel, total),
        out_shape=(jax.ShapeDtypeStruct((rows, k), F32), jax.ShapeDtypeStruct((8, 128), F32)),
        in_specs=[vmem, anywhere],
        out_specs=(anywhere, vmem),
        scratch_shapes=[
            pltpu.VMEM((rows, k), F32),
            pltpu.VMEM((rows, k), F32),
            pltpu.VMEM((k, k), F32),
            dma((n,)),
            dma((n,)),
        ],
        compiler_params=pltpu.CompilerParams(vmem_limit_bytes=VMEM_LIMIT),
        name="invert_and_map",
    )(gram, sketch)
    return basis, logdet[0, 0]


def solution(mesh):
    return jax.shard_map(
        on_device,
        mesh=mesh,
        in_specs=(P(("crow", "ccol"), None),),
        out_specs=(P(("crow", "ccol"), None), P()),
        check_vma=False,
    )
```

time: 387 us -> 74.6 us (0.19)
  waiting for transfers between devices: 150 us -> 0 us
  other arithmetic: 124 us -> 0 us
  Pallas kernels: 0 us -> 72.5 us
  matrix products: 64.8 us -> 0 us
  local copies, waits for them, and re-layouts: 26.1 us -> 1.19 us
  between operations: 19 us -> 0.65 us
    psum x1 -> x0, waiting for transfers between devices: 150 us -> none  [on_device(): summed = lax.psum(partial_value, ('crow', 'ccol'))]
    another operation x18 -> x0, other arithmetic: 119 us -> none  [the longest x14 78.8 us: on_device(): factor = jnp.linalg.cholesky(summed)]
    pallas_call x0 -> x2, Pallas kernels: none -> 72.5 us  [the longest x1 37.6 us: on_device(): pl.pallas_call(functools.partial(map_kernel, total), out_shape=(jax.Shape...]
    dot_general x2 -> x0, matrix products: 49.1 us -> none  [the longest x1 30.3 us: on_device(): jnp.dot(sketch, inverse, precision=lax.Precision.HIGHEST, preferred_eleme...]
    another operation x20 -> x0, matrix products: 15.7 us -> none  [the longest x14 13.3 us: on_device(): jax.scipy.linalg.cho_solve((factor, True), jnp.float32(rows_all) * eye)]
    another operation x38 -> x0, local copies, waits for them, and re-layouts: 12.3 us -> none
    unnamed x1 -> x0, local copies, waits for them, and re-layouts: 8.94 us -> none
    gather x1 -> x0, local copies, waits for them, and re-layouts: 4.55 us -> none  [on_device(): jnp.diagonal(factor)]
  transfers between devices with their start and end apart: 1 -> 0, of which waited for: 1 -> 0; matrix products, arithmetic and copies ran while one was open for 0% -> 0% of each run, Pallas kernels for 0% -> 0%
where the time goes in v1:
time: 74.6 us; the launch traced here: 74.4 us
  Pallas kernels  72.5 us (97%)
  local copies, waits for them, and re-layouts  1.19 us (2%)
    pallas_call x1, Pallas kernels, on_device(): pl.pallas_call(functools.partial(map_kernel, total), out_shape=(jax.Shape...  37.6 us
    pallas_call x1, Pallas kernels, on_device(): pl.pallas_call(gram_kernel, out_shape=jax.ShapeDtypeStruct((2, 64, 8, hal...  34.9 us

profile of v1, /device:TPU:1, one launch (start us, length us, event | category | flops | bytes accessed | tf_op | source)
XLA Modules:
  0.0 74.4 jit_solution(18099077449198627808)
XLA Ops:
  0.6 34.9 %gram_sum.1.gram = f32[2,64,8,256]{3,2,1,0:T(8,128)} custom-call(f32[4096,512]{1,0:T(8,128)} %x_hbm.3), custom_call_target="tpu_custom_call" | custom-call | tf_op jit(solution)/shard_map/gram_sum/pallas_call | solution.py:247
  35.5 37.6 %invert_and_map.1 = (f32[4096,512]{1,0:T(8,128)}, f32[8,128]{1,0:T(8,128)}) custom-call(f32[2,64,8,256]{3,2,1,0:T(8,128)} %gram_sum.1.gram, f32[4096,512]{1,0:T(8,128)} %x_hbm.3), custom_call_target="tpu_custom_call" | custom-call | tf_op jit(solution)/shard_map/invert_and_map/pallas_call | solution.py:271
  73.2 1.2 %slice.3 = f32[1,1]{1,0:T(1,128)} slice(f32[8,128]{1,0:T(8,128)} %get-tuple-element.5), slice={[0:1], [0:1]} | slice | bytes 8 | tf_op jit(solution)/shard_map/slice | solution.py:286

commit v2 on v1

v2 whole, which is shorter than its diff:
```python
import functools

import jax
import jax.numpy as jnp
from jax import lax
from jax.experimental import pallas as pl
from jax.experimental.pallas import tpu as pltpu
from jax.sharding import PartitionSpec as P

MESH = pl.DeviceIdType.MESH
F32, BF16 = jnp.float32, jnp.bfloat16
VMEM_LIMIT = 36 * 2**20
CHUNK = 512
GROUP = 16


def split(x):
    high = x.astype(BF16)
    return high, (x - high.astype(F32)).astype(BF16)


def place():
    crow, ccol = lax.axis_index("crow"), lax.axis_index("ccol")
    return crow // 4, crow % 4, ccol // 2, ccol % 2


def peer(here, offset):
    z, x, y, core = here
    dz, dx, dy = offset
    return (((z + dz) % 4) * 4 + (x + dx) % 4, ((y + dy) % 4) * 2 + core)


def hops(offset):
    return sum(min(d, 4 - d) for d in offset)


OFFSETS = sorted(
    [(dz, dx, dy) for dz in range(4) for dx in range(4) for dy in range(4) if (dz, dx, dy) != (0, 0, 0)],
    key=lambda o: (-hops(o), o),
)


def block_tiles(i, j):
    start = 8 * (i * (i + 1) // 2 + j)
    return slice(start, start + 8)


def first_tile(z, x, s):
    return 5 * (4 * z + x) + s + (s + 2) // 3


def gram_kernel(
    x_hbm, out, high, low, xb, acc, cross, part, crecv, mine, recv,
    load_sem, core_sem, rs_sem, rs2_sem, ag_sem, fw_sem,
):
    rows = x_hbm.shape[0]
    rbuf, rbuf2 = recv.at[pl.ds(0, 63)], recv.at[pl.ds(63, 64)]
    n = rows // CHUNK
    loads = [
        pltpu.make_async_copy(x_hbm.at[pl.ds(i * CHUNK, CHUNK)], xb.at[pl.ds(i * CHUNK, CHUNK)], load_sem.at[i])
        for i in range(n)
    ]
    for load in loads:
        load.start()

    here = place()
    z, x, y, core = here
    s = (x + y + z) % 4
    crow, ccol = lax.axis_index("crow"), lax.axis_index("ccol")
    twin = (crow, ccol + 1 - 2 * core)
    barrier = pltpu.get_barrier_semaphore()
    pl.semaphore_signal(barrier, inc=1, device_id=twin, device_id_type=MESH)
    for offset in OFFSETS:
        pl.semaphore_signal(barrier, inc=1, device_id=peer(here, offset), device_id_type=MESH)

    dims = (((0,), (0,)), ((), ()))
    for i in range(n):
        loads[i].wait()
        span = slice(i * CHUNK, (i + 1) * CHUNK)
        h, l = split(xb[span, :])
        high[span, :] = h
        low[span, :] = l
        a = lax.dot_general(h, h, dims, preferred_element_type=F32)
        b = lax.dot_general(h, l, dims, preferred_element_type=F32)
        if i == 0:
            acc[...] = a
            cross[...] = b
        else:
            acc[...] += a
            cross[...] += b
    for i in range(4):
        for j in range(i + 1):
            si, sj = slice(128 * i, 128 * i + 128), slice(128 * j, 128 * j + 128)
            block = (acc[si, sj] + (cross[si, sj] + cross[sj, si].T)).reshape(8, 2, 8, 128)
            for c in range(2):
                part[c, block_tiles(i, j)] = block[:, c]

    pl.semaphore_wait(barrier, 1 + len(OFFSETS))
    swap = pltpu.make_async_remote_copy(
        src_ref=part.at[1 - core],
        dst_ref=crecv,
        send_sem=core_sem.at[0],
        recv_sem=core_sem.at[1],
        device_id=twin,
        device_id_type=MESH,
    )
    swap.start()
    swap.wait()
    mine[...] = part[core] + crecv[...]

    for slot, offset in enumerate(OFFSETS):
        dz, dx, dy = offset
        tile = first_tile((z + dz) % 4, (x + dx) % 4, (s + dz + dx + dy) % 4)
        pltpu.make_async_remote_copy(
            src_ref=mine.at[tile],
            dst_ref=rbuf.at[slot],
            send_sem=rs_sem.at[0],
            recv_sem=rs_sem.at[1],
            device_id=peer(here, offset),
            device_id_type=MESH,
        ).start()

    def second(dz, dx):
        dy = (12 - s - dz - dx) % 4
        return pltpu.make_async_remote_copy(
            src_ref=mine.at[5 * (((z + dz) % 4) * 4 + (x + dx) % 4) + 1],
            dst_ref=rbuf2.at[16 * dz + 4 * dx + dy],
            send_sem=rs2_sem.at[0],
            recv_sem=rs2_sem.at[1],
            device_id=peer(here, (dz, dx, dy)),
            device_id_type=MESH,
        )

    for dz in (2, 1, 3, 0):
        for dx in (2, 1, 3, 0):
            if (dz, dx) != (0, 0):
                second(dz, dx).start()

    @pl.when(s != 0)
    def _():
        second(0, 0).start()

    def summed(values):
        while len(values) > 1:
            values = [a + b for a, b in zip(values[0::2], values[1::2])]
        return values[0]

    tile = first_tile(z, x, s)
    pltpu.make_async_copy(rbuf, rbuf, rs_sem.at[1]).wait()
    out[core, tile] = summed([mine[tile]] + [rbuf[slot] for slot in range(63)])

    def gather(count):
        for offset in OFFSETS:
            pltpu.make_async_remote_copy(
                src_ref=out.at[core, pl.ds(tile, count)],
                dst_ref=out.at[core, pl.ds(tile, count)],
                send_sem=ag_sem.at[0],
                recv_sem=ag_sem.at[1],
                device_id=peer(here, offset),
                device_id_type=MESH,
            ).start()
        rest = out.at[core, pl.ds(0, 80 - count)]
        pltpu.make_async_copy(rest, rest, ag_sem.at[1]).wait()

    @pl.when(s == 0)
    def _():
        others = rbuf2.at[pl.ds(1, 63)]
        pltpu.make_async_copy(others, others, rs2_sem.at[1]).wait()
        out[core, tile + 1] = summed([mine[tile + 1]] + [rbuf2[slot] for slot in range(1, 64)])
        gather(2)

    @pl.when(s != 0)
    def _():
        gather(1)

    forward = pltpu.make_async_remote_copy(
        src_ref=out.at[core],
        dst_ref=out.at[core],
        send_sem=fw_sem.at[0],
        recv_sem=fw_sem.at[1],
        device_id=twin,
        device_id_type=MESH,
    )
    forward.start()
    pltpu.make_async_copy(rbuf, rbuf, rs_sem.at[0]).wait()

    @pl.when(s == 0)
    def _():
        sent, both = rbuf2.at[pl.ds(0, 15)], recv.at[pl.ds(0, 126)]
        pltpu.make_async_copy(sent, sent, rs2_sem.at[0]).wait()
        pltpu.make_async_copy(both, both, ag_sem.at[0]).wait()

    @pl.when(s != 0)
    def _():
        sent = rbuf2.at[pl.ds(0, 16)]
        pltpu.make_async_copy(sent, sent, rs2_sem.at[0]).wait()
        pltpu.make_async_copy(rbuf, rbuf, ag_sem.at[0]).wait()

    forward.wait()


def sub_row(x, s):
    return jnp.broadcast_to(x[s : s + 1, :], (8, 128))


def lane_col(x, j):
    return jnp.broadcast_to(x[:, j : j + 1], (8, 128))


def invert_leaf(rows):
    lane = lax.broadcasted_iota(jnp.int32, (8, 128), 1)
    sub = lax.broadcasted_iota(jnp.int32, (8, 128), 0)
    rows = list(rows)
    dets = jnp.ones((8, 128), F32)
    zero = jnp.zeros((8, 128), F32)
    nv = GROUP // 8
    for g in range(128 // GROUP):
        a = GROUP * g
        own = [nv * g + v for v in range(nv)]
        near = [i for i in range(own[-1] + 1, own[-1] + 1 + nv) if i < 16]
        cols = [[lane_col(rows[m], a + j) for m in own] for j in range(GROUP)]
        left = {i: [lane_col(rows[i], a + j) for j in range(GROUP)] for i in near}
        inside = (lane >= a) & (lane < a + GROUP)
        top = [jnp.where(inside, (lane - a == sub + 8 * v).astype(F32), rows[m]) for v, m in enumerate(own)]
        diag, off = [zero] * nv, [zero] * nv
        for k in range(0, GROUP, 2):
            v0, s0 = divmod(k, 8)
            c0, c1 = cols[k], cols[k + 1]
            p00, p10 = sub_row(c0[v0], s0), sub_row(c0[v0], s0 + 1)
            p01, p11 = sub_row(c1[v0], s0), sub_row(c1[v0], s0 + 1)
            det = p00 * p11 - p01 * p10
            r = 1.0 / det
            dets = jnp.where(lane == a + k, det, dets)
            diag[v0] = jnp.where(sub == s0, p11 * r, jnp.where(sub == s0 + 1, p00 * r, diag[v0]))
            off[v0] = jnp.where(sub == s0, -p01 * r, jnp.where(sub == s0 + 1, -p10 * r, off[v0]))
            n0 = [c0[v] * p11 - c1[v] * p10 for v in range(nv)]
            n1 = [c1[v] * p00 - c0[v] * p01 for v in range(nv)]
            pair = (sub == s0) | (sub == s0 + 1)
            n0[v0] = jnp.where(pair, 0.0, n0[v0])
            n1[v0] = jnp.where(pair, 0.0, n1[v0])
            f0, f1 = [n * r for n in n0], [n * r for n in n1]
            for j in range(k + 2, GROUP):
                b0, b1 = sub_row(cols[j][v0], s0), sub_row(cols[j][v0], s0 + 1)
                if j < k + 4:
                    cols[j] = [cols[j][v] - (n0[v] * b0 + n1[v] * b1) * r for v in range(nv)]
                else:
                    cols[j] = [cols[j][v] - (f0[v] * b0 + f1[v] * b1) for v in range(nv)]
            b0, b1 = sub_row(top[v0], s0), sub_row(top[v0], s0 + 1)
            top = [top[v] - (f0[v] * b0 + f1[v] * b1) for v in range(nv)]
        swapped = [jnp.where(sub % 2 == 0, pltpu.roll(t, 7, 0), pltpu.roll(t, 1, 0)) for t in top]
        top = [diag[v] * top[v] + off[v] * swapped[v] for v in range(nv)]
        spread = [sub_row(top[j // 8], j % 8) for j in range(GROUP)]
        new = dict(zip(own, top))
        for i in near:
            terms = [left[i][j] * spread[j] for j in range(GROUP)]
            while len(terms) > 1:
                terms = [s + t for s, t in zip(terms[0::2], terms[1::2])]
            new[i] = jnp.where(inside, 0.0, rows[i]) - terms[0]
        padded = [jnp.zeros((a, 128), F32)] * (a > 0) + top + [jnp.zeros((128 - a - GROUP, 128), F32)] * (a + GROUP < 128)
        padded = jnp.concatenate(padded, axis=0)
        for start, stop in ((0, own[0]), (own[-1] + 1 + len(near), 16)):
            if stop > start:
                update = dot_exact(jnp.concatenate(rows[start:stop], axis=0), padded)
                for i in range(start, stop):
                    new[i] = jnp.where(inside, 0.0, rows[i]) - update[8 * (i - start) : 8 * (i - start) + 8]
        rows = [new[i] for i in range(16)]
    return rows, dets


def dot_exact(a, b):
    return jnp.dot(a, b, precision=lax.Precision.HIGHEST, preferred_element_type=F32)


def map_kernel(total, gram, high, low, out_hbm, logdet, ob, mat, store_sem):
    rows, k = high.shape
    n = rows // CHUNK
    eye = lax.broadcasted_iota(jnp.int32, (128, 128), 0) == lax.broadcasted_iota(jnp.int32, (128, 128), 1)
    for i in range(k // 128):
        for j in range(i + 1):
            tiles = block_tiles(i, j)
            block = jnp.stack([gram[0, tiles], gram[1, tiles]], axis=1).reshape(128, 128) * (1.0 / total)
            if i == j:
                block = block + eye.astype(F32)
            else:
                mat[128 * j : 128 * j + 128, 128 * i : 128 * i + 128] = block.T
            mat[128 * i : 128 * i + 128, 128 * j : 128 * j + 128] = block

    logs = jnp.zeros((8, 128), F32)
    count = k // 128
    block = mat[:128, :128]
    for b in range(count):
        lo, hi = 128 * b, 128 * (b + 1)
        leaf, dets = invert_leaf([block[8 * i : 8 * i + 8] for i in range(16)])
        logs = logs + jnp.log(dets)
        inverse = jnp.concatenate(leaf, axis=0)
        sides = [mat[128 * i : 128 * i + 128, lo:hi] for i in range(count)]
        if b + 1 < count:
            first = dot_exact(inverse, mat[lo:hi, hi : hi + 128])
            block = mat[hi : hi + 128, hi : hi + 128] - dot_exact(sides[b + 1], first)
        parts = []
        if lo:
            parts.append(dot_exact(inverse, mat[lo:hi, :lo]))
        parts.append(inverse)
        if b + 1 < count:
            parts.append(first)
        if hi + 128 < k:
            parts.append(dot_exact(inverse, mat[lo:hi, hi + 128 :]))
        top = jnp.concatenate(parts, axis=1)
        for i in range(count):
            if i != b:
                update = dot_exact(sides[i], top)
                for j in range(count):
                    rows_i, cols_j = slice(128 * i, 128 * i + 128), slice(128 * j, 128 * j + 128)
                    if j == b:
                        mat[rows_i, cols_j] = -update[:, cols_j]
                    else:
                        mat[rows_i, cols_j] -= update[:, cols_j]
        mat[lo:hi, :] = top
    logdet[0, 0] = jnp.sum(logs[0:1, :]) * (1.0 / k)

    mh, ml = split(mat[...])
    stores = []
    for i in range(n):
        span = slice(i * CHUNK, (i + 1) * CHUNK)
        xh = high[span, :]
        y = jnp.dot(low[span, :], mh, preferred_element_type=F32) + jnp.dot(xh, ml, preferred_element_type=F32)
        ob[span, :] = jnp.dot(xh, mh, preferred_element_type=F32) + y
        store = pltpu.make_async_copy(
            ob.at[pl.ds(i * CHUNK, CHUNK)], out_hbm.at[pl.ds(i * CHUNK, CHUNK)], store_sem.at[i]
        )
        store.start()
        stores.append(store)
    for store in stores:
        store.wait()


VMEM, HBM = pl.BlockSpec(memory_space=pltpu.VMEM), pl.BlockSpec(memory_space=pltpu.HBM)
DMA = pltpu.SemaphoreType.DMA


def gram_sum(sketch):
    rows, k = sketch.shape
    return pl.pallas_call(
        gram_kernel,
        out_shape=(
            jax.ShapeDtypeStruct((2, 80, 8, 128), F32),
            jax.ShapeDtypeStruct((rows, k), BF16),
            jax.ShapeDtypeStruct((rows, k), BF16),
        ),
        in_specs=[HBM],
        out_specs=(VMEM, VMEM, VMEM),
        scratch_shapes=[
            pltpu.VMEM((rows, k), F32),
            pltpu.VMEM((k, k), F32),
            pltpu.VMEM((k, k), F32),
            pltpu.VMEM((2, 80, 8, 128), F32),
            pltpu.VMEM((80, 8, 128), F32),
            pltpu.VMEM((80, 8, 128), F32),
            pltpu.VMEM((127, 8, 128), F32),
            DMA((rows // CHUNK,)),
            DMA((2,)),
            DMA((2,)),
            DMA((2,)),
            DMA((2,)),
            DMA((2,)),
        ],
        compiler_params=pltpu.CompilerParams(
            collective_id=0, has_side_effects=True, vmem_limit_bytes=VMEM_LIMIT
        ),
        name="gram_sum",
    )(sketch)


def invert_and_map(gram, high, low, total):
    rows, k = high.shape
    return pl.pallas_call(
        functools.partial(map_kernel, total),
        out_shape=(jax.ShapeDtypeStruct((rows, k), F32), jax.ShapeDtypeStruct((1, 1), F32)),
        in_specs=[VMEM, VMEM, VMEM],
        out_specs=(HBM, pl.BlockSpec(memory_space=pltpu.SMEM)),
        scratch_shapes=[
            pltpu.VMEM((rows, k), F32),
            pltpu.VMEM((k, k), F32),
            DMA((rows // CHUNK,)),
        ],
        compiler_params=pltpu.CompilerParams(vmem_limit_bytes=VMEM_LIMIT),
        name="invert_and_map",
    )(gram, high, low)


def on_device(sketch):
    total = sketch.shape[0] * lax.axis_size("crow") * lax.axis_size("ccol")
    basis, logdet = invert_and_map(*gram_sum(pltpu.with_memory_space_constraint(sketch, pltpu.HBM)), total)
    return basis, logdet.reshape(())


def solution(mesh):
    return jax.shard_map(
        on_device,
        mesh=mesh,
        in_specs=(P(("crow", "ccol"), None),),
        out_specs=(P(("crow", "ccol"), None), P()),
        check_vma=False,
    )
```

time: 74.6 us -> 55.3 us (0.74)
  Pallas kernels: 72.5 us -> 54.4 us
  local copies, waits for them, and re-layouts: 1.19 us -> 0 us
    pallas_call x2, Pallas kernels: 72.5 us -> 54.4 us  [the longest x1 31.7 us: gram_sum(): pl.pallas_call(gram_kernel, out_shape=(jax.ShapeDtypeStruct((2, 80, 8, 12...]
    slice x1 -> x0, local copies, waits for them, and re-layouts: 1.19 us -> none  [on_device(): return (basis, logdet[0, 0])]
where the time goes in v2:
time: 55.3 us; the launch traced here: 55.2 us
  Pallas kernels  54.4 us (98%)
  between operations  0.82 us (1%)
    pallas_call x1, Pallas kernels, gram_sum(): pl.pallas_call(gram_kernel, out_shape=(jax.ShapeDtypeStruct((2, 80, 8, 12...  31.7 us
    pallas_call x1, Pallas kernels, invert_and_map(): pl.pallas_call(functools.partial(map_kernel, total), out_shape=(jax.Shape...  22.7 us

profile of v2, /device:TPU:1, one launch (start us, length us, event | category | flops | bytes accessed | tf_op | source)
XLA Modules:
  0.0 55.2 jit_solution(4273998279239147812)
XLA Ops:
  0.6 31.7 %gram_sum.1 = (f32[2,80,8,128]{3,2,1,0:T(8,128)S(1)}, bf16[4096,512]{1,0:T(8,128)(2,1)S(1)}, bf16[4096,512]{1,0:T(8,128)(2,1)S(1)}) custom-call(f32[4096,512]{1,0:T(8,128)} %x_hbm.1), custom_call_target="tpu_custom_call" | custom-call | tf_op jit(solution)/shard_map/gram_sum/pallas_call | solution.py:343
  32.3 22.7 %invert_and_map.1 = (f32[4096,512]{1,0:T(8,128)}, f32[1,1]{1,0:T(1,128)}) custom-call(f32[2,80,8,128]{3,2,1,0:T(8,128)S(1)} %get-tuple-element.7.gram, bf16[4096,512]{1,0:T(8,128)(2,1)S(1)} %get-tuple-element.8.high, bf16[4096,512]{1,0:T(8,128)(2,1)S(1)} %get-tuple-element.9.low), custom_call_target="tpu_custom_call" | custom-call | tf_op jit(solution)/shard_map/invert_and_map/pallas_call | solution.py:376

commit v3 on v2

--- a/solution.py
+++ b/solution.py
@@ -11,7 +11,9 @@
 F32, BF16 = jnp.float32, jnp.bfloat16
 VMEM_LIMIT = 36 * 2**20
 CHUNK = 512
+STORE = 256
 GROUP = 16
+FORWARD_AFTER = 5
 
 
 def split(x):
@@ -45,13 +47,18 @@
     return slice(start, start + 8)
 
 
-def first_tile(z, x, s):
-    return 5 * (4 * z + x) + s + (s + 2) // 3
+def load_block(tiles_ref, i, j, total):
+    tiles = block_tiles(i, j)
+    return jnp.stack([tiles_ref[0, tiles], tiles_ref[1, tiles]], axis=1).reshape(128, 128) * (1.0 / total)
+
+
+def unit(n):
+    return (lax.broadcasted_iota(jnp.int32, (n, n), 0) == lax.broadcasted_iota(jnp.int32, (n, n), 1)).astype(F32)
 
 
 def gram_kernel(
-    x_hbm, out, high, low, xb, acc, cross, part, crecv, mine, recv,
-    load_sem, core_sem, rs_sem, rs2_sem, ag_sem, fw_sem,
+    total, x_hbm, out, high, low, inverse, first, dets, xb, acc, cross, part, crecv, mine, recv,
+    load_sem, core_sem, rs_sem, rs2_sem, ag_sem, ag2_sem, fw_sem, fw2_sem,
 ):
     rows = x_hbm.shape[0]
     rbuf, rbuf2 = recv.at[pl.ds(0, 63)], recv.at[pl.ds(63, 64)]
@@ -108,11 +115,30 @@
     swap.wait()
     mine[...] = part[core] + crecv[...]
 
+    def second(dz, dx):
+        dy = (12 - s - dz - dx) % 4
+        return pltpu.make_async_remote_copy(
+            src_ref=mine.at[((z + dz) % 4) * 4 + (x + dx) % 4],
+            dst_ref=rbuf2.at[16 * dz + 4 * dx + dy],
+            send_sem=rs2_sem.at[0],
+            recv_sem=rs2_sem.at[1],
+            device_id=peer(here, (dz, dx, dy)),
+            device_id_type=MESH,
+        )
+
+    for dz in (2, 1, 3, 0):
+        for dx in (2, 1, 3, 0):
+            if (dz, dx) != (0, 0):
+                second(dz, dx).start()
+
+    @pl.when(s != 0)
+    def _():
+        second(0, 0).start()
+
     for slot, offset in enumerate(OFFSETS):
         dz, dx, dy = offset
-        tile = first_tile((z + dz) % 4, (x + dx) % 4, (s + dz + dx + dy) % 4)
         pltpu.make_async_remote_copy(
-            src_ref=mine.at[tile],
+            src_ref=mine.at[16 + (((z + dz) % 4) * 4 + (x + dx) % 4) * 4 + (y + dy) % 4],
             dst_ref=rbuf.at[slot],
             send_sem=rs_sem.at[0],
             recv_sem=rs_sem.at[1],
@@ -120,83 +146,85 @@
             device_id_type=MESH,
         ).start()
 
-    def second(dz, dx):
-        dy = (12 - s - dz - dx) % 4
-        return pltpu.make_async_remote_copy(
-            src_ref=mine.at[5 * (((z + dz) % 4) * 4 + (x + dx) % 4) + 1],
-            dst_ref=rbuf2.at[16 * dz + 4 * dx + dy],
-            send_sem=rs2_sem.at[0],
-            recv_sem=rs2_sem.at[1],
-            device_id=peer(here, (dz, dx, dy)),
-            device_id_type=MESH,
-        )
-
-    for dz in (2, 1, 3, 0):
-        for dx in (2, 1, 3, 0):
-            if (dz, dx) != (0, 0):
-                second(dz, dx).start()
-
-    @pl.when(s != 0)
-    def _():
-        second(0, 0).start()
-
     def summed(values):
         while len(values) > 1:
             values = [a + b for a, b in zip(values[0::2], values[1::2])]
         return values[0]
 
-    tile = first_tile(z, x, s)
-    pltpu.make_async_copy(rbuf, rbuf, rs_sem.at[1]).wait()
-    out[core, tile] = summed([mine[tile]] + [rbuf[slot] for slot in range(63)])
-
-    def gather(count):
+    def gather(tile, sem):
         for offset in OFFSETS:
             pltpu.make_async_remote_copy(
-                src_ref=out.at[core, pl.ds(tile, count)],
-                dst_ref=out.at[core, pl.ds(tile, count)],
-                send_sem=ag_sem.at[0],
-                recv_sem=ag_sem.at[1],
+                src_ref=out.at[core, tile],
+                dst_ref=out.at[core, tile],
+                send_sem=sem.at[0],
+                recv_sem=sem.at[1],
                 device_id=peer(here, offset),
                 device_id_type=MESH,
             ).start()
-        rest = out.at[core, pl.ds(0, 80 - count)]
-        pltpu.make_async_copy(rest, rest, ag_sem.at[1]).wait()
+
+    def forward(tiles, sem):
+        return pltpu.make_async_remote_copy(
+            src_ref=out.at[core, tiles],
+            dst_ref=out.at[core, tiles],
+            send_sem=sem.at[0],
+            recv_sem=sem.at[1],
+            device_id=twin,
+            device_id_type=MESH,
+        )
+
+    def settle(ref, sem):
+        pltpu.make_async_copy(ref, ref, sem).wait()
 
     @pl.when(s == 0)
     def _():
-        others = rbuf2.at[pl.ds(1, 63)]
-        pltpu.make_async_copy(others, others, rs2_sem.at[1]).wait()
-        out[core, tile + 1] = summed([mine[tile + 1]] + [rbuf2[slot] for slot in range(1, 64)])
-        gather(2)
+        settle(rbuf2.at[pl.ds(1, 63)], rs2_sem.at[1])
+        out[core, 4 * z + x] = summed([mine[4 * z + x]] + [rbuf2[slot] for slot in range(1, 64)])
+        gather(4 * z + x, ag2_sem)
+
+    chip = (z * 4 + x) * 4 + y
+    settle(rbuf, rs_sem.at[1])
+    out[core, 16 + chip] = summed([mine[16 + chip]] + [rbuf[slot] for slot in range(63)])
+    gather(16 + chip, ag_sem)
+
+    @pl.when(s == 0)
+    def _():
+        settle(rbuf2.at[pl.ds(0, 15)], ag2_sem.at[1])
 
     @pl.when(s != 0)
     def _():
-        gather(1)
-
-    forward = pltpu.make_async_remote_copy(
-        src_ref=out.at[core],
-        dst_ref=out.at[core],
-        send_sem=fw_sem.at[0],
-        recv_sem=fw_sem.at[1],
-        device_id=twin,
-        device_id_type=MESH,
-    )
-    forward.start()
-    pltpu.make_async_copy(rbuf, rbuf, rs_sem.at[0]).wait()
+        settle(rbuf2.at[pl.ds(0, 16)], ag2_sem.at[1])
+
+    ahead = forward(pl.ds(0, 16), fw2_sem)
+    ahead.start()
+    ahead.wait_recv()
+    later = forward(pl.ds(16, 64), fw_sem)
+    calls = iter(range(8))
+
+    def between():
+        if next(calls) == FORWARD_AFTER:
+            settle(rbuf, ag_sem.at[1])
+            later.start()
+
+    block = load_block(out, 0, 0, total) + unit(128)
+    leaf, dets[...] = invert_leaf([block[8 * i : 8 * i + 8] for i in range(16)], between)
+    leaf = jnp.concatenate(leaf, axis=0)
+    inverse[...] = leaf
+    first[...] = dot_exact(leaf, load_block(out, 1, 0, total).T)
+
+    settle(rbuf, rs_sem.at[0])
+    settle(rbuf, ag_sem.at[0])
 
     @pl.when(s == 0)
     def _():
-        sent, both = rbuf2.at[pl.ds(0, 15)], recv.at[pl.ds(0, 126)]
-        pltpu.make_async_copy(sent, sent, rs2_sem.at[0]).wait()
-        pltpu.make_async_copy(both, both, ag_sem.at[0]).wait()
+        settle(rbuf2.at[pl.ds(0, 15)], rs2_sem.at[0])
+        settle(rbuf, ag2_sem.at[0])
 
     @pl.when(s != 0)
     def _():
-        sent = rbuf2.at[pl.ds(0, 16)]
-        pltpu.make_async_copy(sent, sent, rs2_sem.at[0]).wait()
-        pltpu.make_async_copy(rbuf, rbuf, ag_sem.at[0]).wait()
-
-    forward.wait()
+        settle(rbuf2.at[pl.ds(0, 16)], rs2_sem.at[0])
+
+    ahead.wait_send()
+    later.wait()
 
 
 def sub_row(x, s):
@@ -207,7 +235,7 @@
     return jnp.broadcast_to(x[:, j : j + 1], (8, 128))
 
 
-def invert_leaf(rows):
+def invert_leaf(rows, between):
     lane = lax.broadcasted_iota(jnp.int32, (8, 128), 1)
     sub = lax.broadcasted_iota(jnp.int32, (8, 128), 0)
     rows = list(rows)
@@ -264,6 +292,7 @@
                 for i in range(start, stop):
                     new[i] = jnp.where(inside, 0.0, rows[i]) - update[8 * (i - start) : 8 * (i - start) + 8]
         rows = [new[i] for i in range(16)]
+        between()
     return rows, dets
 
 
@@ -271,62 +300,87 @@
     return jnp.dot(a, b, precision=lax.Precision.HIGHEST, preferred_element_type=F32)
 
 
-def map_kernel(total, gram, high, low, out_hbm, logdet, ob, mat, store_sem):
+def dot3(a, b):
+    (ah, al), (bh, bl) = a, b
+    small = jnp.dot(al, bh, preferred_element_type=F32) + jnp.dot(ah, bl, preferred_element_type=F32)
+    return jnp.dot(ah, bh, preferred_element_type=F32) + small
+
+
+def map_kernel(total, gram, high, low, inverse0, first0, dets0, out_hbm, logdet, ob, zh, zl, mat, store_sem):
     rows, k = high.shape
     n = rows // CHUNK
-    eye = lax.broadcasted_iota(jnp.int32, (128, 128), 0) == lax.broadcasted_iota(jnp.int32, (128, 128), 1)
     for i in range(k // 128):
         for j in range(i + 1):
-            tiles = block_tiles(i, j)
-            block = jnp.stack([gram[0, tiles], gram[1, tiles]], axis=1).reshape(128, 128) * (1.0 / total)
+            block = load_block(gram, i, j, total)
             if i == j:
-                block = block + eye.astype(F32)
+                block = block + unit(128)
             else:
                 mat[128 * j : 128 * j + 128, 128 * i : 128 * i + 128] = block.T
             mat[128 * i : 128 * i + 128, 128 * j : 128 * j + 128] = block
 
-    logs = jnp.zeros((8, 128), F32)
-    count = k // 128
-    block = mat[:128, :128]
+    half, count = k // 2, k // 128
+    early = iter(range(n))
+    weights = []
+
+    def forward_chunk():
+        i = next(early, None)
+        if i is None:
+            return
+        if not weights:
+            weights.extend(split(mat[:half, :]))
+        span = slice(i * CHUNK, (i + 1) * CHUNK)
+        d = dot3((high[span, :half], low[span, :half]), weights)
+        ob[span, :half] = d[:, :half]
+        zh[span, :], zl[span, :] = split((high[span, half:].astype(F32) + low[span, half:].astype(F32)) - d[:, half:])
+
+    logs = jnp.log(dets0[...])
     for b in range(count):
         lo, hi = 128 * b, 128 * (b + 1)
-        leaf, dets = invert_leaf([block[8 * i : 8 * i + 8] for i in range(16)])
-        logs = logs + jnp.log(dets)
-        inverse = jnp.concatenate(leaf, axis=0)
-        sides = [mat[128 * i : 128 * i + 128, lo:hi] for i in range(count)]
+        base = 0 if lo < half else half
+        if b == 0:
+            inverse = inverse0[...]
+        else:
+            leaf, dets = invert_leaf(
+                [block[8 * i : 8 * i + 8] for i in range(16)], forward_chunk if base else lambda: None
+            )
+            logs = logs + jnp.log(dets)
+            inverse = jnp.concatenate(leaf, axis=0)
+        sides = {i: mat[128 * i : 128 * i + 128, lo:hi] for i in range(base // 128, count)}
         if b + 1 < count:
-            first = dot_exact(inverse, mat[lo:hi, hi : hi + 128])
+            first = dot_exact(inverse, mat[lo:hi, hi : hi + 128]) if b else first0[...]
             block = mat[hi : hi + 128, hi : hi + 128] - dot_exact(sides[b + 1], first)
         parts = []
-        if lo:
-            parts.append(dot_exact(inverse, mat[lo:hi, :lo]))
+        if lo > base:
+            parts.append(dot_exact(inverse, mat[lo:hi, base:lo]))
         parts.append(inverse)
         if b + 1 < count:
             parts.append(first)
         if hi + 128 < k:
             parts.append(dot_exact(inverse, mat[lo:hi, hi + 128 :]))
         top = jnp.concatenate(parts, axis=1)
-        for i in range(count):
+        for i in sides:
             if i != b:
                 update = dot_exact(sides[i], top)
-                for j in range(count):
+                for j in sides:
                     rows_i, cols_j = slice(128 * i, 128 * i + 128), slice(128 * j, 128 * j + 128)
+                    change = update[:, 128 * j - base : 128 * j - base + 128]
                     if j == b:
-                        mat[rows_i, cols_j] = -update[:, cols_j]
+                        mat[rows_i, cols_j] = -change
                     else:
-                        mat[rows_i, cols_j] -= update[:, cols_j]
-        mat[lo:hi, :] = top
+                        mat[rows_i, cols_j] -= change
+        mat[lo:hi, base:] = top
     logdet[0, 0] = jnp.sum(logs[0:1, :]) * (1.0 / k)
 
-    mh, ml = split(mat[...])
+    tail = split(mat[half:, half:])
+    back = split(dot_exact(mat[half:, half:], mat[half:, :half]))
     stores = []
-    for i in range(n):
-        span = slice(i * CHUNK, (i + 1) * CHUNK)
-        xh = high[span, :]
-        y = jnp.dot(low[span, :], mh, preferred_element_type=F32) + jnp.dot(xh, ml, preferred_element_type=F32)
-        ob[span, :] = jnp.dot(xh, mh, preferred_element_type=F32) + y
+    for i in range(rows // STORE):
+        span = slice(i * STORE, (i + 1) * STORE)
+        z = zh[span, :], zl[span, :]
+        ob[span, half:] = dot3(z, tail)
+        ob[span, :half] += dot3(z, back)
         store = pltpu.make_async_copy(
-            ob.at[pl.ds(i * CHUNK, CHUNK)], out_hbm.at[pl.ds(i * CHUNK, CHUNK)], store_sem.at[i]
+            ob.at[pl.ds(i * STORE, STORE)], out_hbm.at[pl.ds(i * STORE, STORE)], store_sem.at[i]
         )
         store.start()
         stores.append(store)
@@ -338,17 +392,20 @@
 DMA = pltpu.SemaphoreType.DMA
 
 
-def gram_sum(sketch):
+def gram_sum(sketch, total):
     rows, k = sketch.shape
     return pl.pallas_call(
-        gram_kernel,
+        functools.partial(gram_kernel, total),
         out_shape=(
             jax.ShapeDtypeStruct((2, 80, 8, 128), F32),
             jax.ShapeDtypeStruct((rows, k), BF16),
             jax.ShapeDtypeStruct((rows, k), BF16),
+            jax.ShapeDtypeStruct((128, 128), F32),
+            jax.ShapeDtypeStruct((128, 128), F32),
+            jax.ShapeDtypeStruct((8, 128), F32),
         ),
         in_specs=[HBM],
-        out_specs=(VMEM, VMEM, VMEM),
+        out_specs=(VMEM,) * 6,
         scratch_shapes=[
             pltpu.VMEM((rows, k), F32),
             pltpu.VMEM((k, k), F32),
@@ -358,39 +415,37 @@
             pltpu.VMEM((80, 8, 128), F32),
             pltpu.VMEM((127, 8, 128), F32),
             DMA((rows // CHUNK,)),
-            DMA((2,)),
-            DMA((2,)),
-            DMA((2,)),
-            DMA((2,)),
-            DMA((2,)),
-        ],
+        ]
+        + [DMA((2,))] * 7,
         compiler_params=pltpu.CompilerParams(
             collective_id=0, has_side_effects=True, vmem_limit_bytes=VMEM_LIMIT
         ),
         name="gram_sum",
-    )(sketch)
-
-
-def invert_and_map(gram, high, low, total):
+    )(pltpu.with_memory_space_constraint(sketch, pltpu.HBM))
+
+
+def invert_and_map(total, gram, high, low, inverse, first, dets):
     rows, k = high.shape
     return pl.pallas_call(
         functools.partial(map_kernel, total),
         out_shape=(jax.ShapeDtypeStruct((rows, k), F32), jax.ShapeDtypeStruct((1, 1), F32)),
-        in_specs=[VMEM, VMEM, VMEM],
+        in_specs=[VMEM] * 6,
         out_specs=(HBM, pl.BlockSpec(memory_space=pltpu.SMEM)),
         scratch_shapes=[
             pltpu.VMEM((rows, k), F32),
+            pltpu.VMEM((rows, k // 2), BF16),
+            pltpu.VMEM((rows, k // 2), BF16),
             pltpu.VMEM((k, k), F32),
-            DMA((rows // CHUNK,)),
+            DMA((rows // STORE,)),
         ],
         compiler_params=pltpu.CompilerParams(vmem_limit_bytes=VMEM_LIMIT),
         name="invert_and_map",
-    )(gram, high, low)
+    )(gram, high, low, inverse, first, dets)
 
 
 def on_device(sketch):
     total = sketch.shape[0] * lax.axis_size("crow") * lax.axis_size("ccol")
-    basis, logdet = invert_and_map(*gram_sum(pltpu.with_memory_space_constraint(sketch, pltpu.HBM)), total)
+    basis, logdet = invert_and_map(total, *gram_sum(sketch, total))
     return basis, logdet.reshape(())
 
 

time: 55.3 us -> 51.2 us (0.926)
  Pallas kernels: 54.4 us -> 50.2 us
    pallas_call x1, Pallas kernels: 22.7 us -> 17.8 us  [invert_and_map(): pl.pallas_call(functools.partial(map_kernel, total), out_shape=(jax.Shape...]
    pallas_call x1, Pallas kernels: 31.7 us -> 32.4 us  [gram_sum(): pl.pallas_call(functools.partial(gram_kernel, total), out_shape=(jax.Shap...]
where the time goes in v3:
time: 51.2 us; the launch traced here: 51.1 us
  Pallas kernels  50.2 us (98%)
  between operations  0.82 us (2%)
    pallas_call x1, Pallas kernels, gram_sum(): pl.pallas_call(functools.partial(gram_kernel, total), out_shape=(jax.Shap...  32.4 us
    pallas_call x1, Pallas kernels, invert_and_map(): pl.pallas_call(functools.partial(map_kernel, total), out_shape=(jax.Shape...  17.8 us

profile of v3, /device:TPU:1, one launch (start us, length us, event | category | flops | bytes accessed | tf_op | source)
XLA Modules:
  0.0 51.1 jit_solution(5878180845157246314)
XLA Ops:
  0.6 32.4 %gram_sum.1 = (f32[2,80,8,128]{3,2,1,0:T(8,128)S(1)}, bf16[4096,512]{1,0:T(8,128)(2,1)S(1)}, bf16[4096,512]{1,0:T(8,128)(2,1)S(1)}, f32[128,128]{1,0:T(8,128)S(1...) custom-call(f32[4096,512]{1,0:T(8,128)} %x_hbm.1), custom_call_target="tpu_custom_call" | custom-call | tf_op jit(solution)/shard_map/gram_sum/pallas_call | solution.py:397
  33.1 17.8 %invert_and_map.1 = (f32[4096,512]{1,0:T(8,128)}, f32[1,1]{1,0:T(1,128)}) custom-call(f32[2,80,8,128]{3,2,1,0:T(8,128)S(1)} %get-tuple-element.10.gram, bf16[4096,512]{1,0:T(8,128)(2,1)S(1)} %get-tuple-element.11.high, bf16[4096,512]{1,0:T(8,128)(2,1)S(1)} %get-tuple-element.12.low, f32[128,128]{1,0:T(8,128)S(1)} %get-tuple-element.13.inverse0, ...), custom_call_target="tpu_custom_call" | custom-call | tf_op jit(solution)/shard_map/invert_and_map/pallas_call | solution.py:429

commit v4 on v3

--- a/solution.py
+++ b/solution.py
@@ -13,7 +13,7 @@
 CHUNK = 512
 STORE = 256
 GROUP = 16
-FORWARD_AFTER = 5
+FORWARD_AFTER = 6
 
 
 def split(x):
@@ -26,10 +26,10 @@
     return crow // 4, crow % 4, ccol // 2, ccol % 2
 
 
-def peer(here, offset):
+def peer(here, offset, other=False):
     z, x, y, core = here
     dz, dx, dy = offset
-    return (((z + dz) % 4) * 4 + (x + dx) % 4, ((y + dy) % 4) * 2 + core)
+    return (((z + dz) % 4) * 4 + (x + dx) % 4, ((y + dy) % 4) * 2 + (1 - core if other else core))
 
 
 def hops(offset):
@@ -42,6 +42,19 @@
 )
 
 
+def opposite(offset):
+    return tuple((d + 2) % 4 for d in offset)
+
+
+NEAR = [o for o in OFFSETS if (hops(o), o) < (hops(opposite(o)), opposite(o))]
+EARLY = 32
+
+
+def early_tile(z, x, s):
+    flip = 2 * (s // 2)
+    return 4 * ((z + flip) % 4) + (x + flip) % 4 + 16 * (s % 2)
+
+
 def block_tiles(i, j):
     start = 8 * (i * (i + 1) // 2 + j)
     return slice(start, start + 8)
@@ -57,8 +70,8 @@
 
 
 def gram_kernel(
-    total, x_hbm, out, high, low, inverse, first, dets, xb, acc, cross, part, crecv, mine, recv,
-    load_sem, core_sem, rs_sem, rs2_sem, ag_sem, ag2_sem, fw_sem, fw2_sem,
+    total, x_hbm, out, high, low, inverse0, first0, inverse1, dets, xb, acc, cross, part, crecv, mine, recv,
+    load_sem, swap_sem, swap2_sem, rs_sem, rs2_sem, ag_sem, ag2_sem, fw_sem,
 ):
     rows = x_hbm.shape[0]
     rbuf, rbuf2 = recv.at[pl.ds(0, 63)], recv.at[pl.ds(63, 64)]
@@ -73,13 +86,17 @@
     here = place()
     z, x, y, core = here
     s = (x + y + z) % 4
-    crow, ccol = lax.axis_index("crow"), lax.axis_index("ccol")
-    twin = (crow, ccol + 1 - 2 * core)
+    twin = peer(here, (0, 0, 0), True)
     barrier = pltpu.get_barrier_semaphore()
-    pl.semaphore_signal(barrier, inc=1, device_id=twin, device_id_type=MESH)
-    for offset in OFFSETS:
-        pl.semaphore_signal(barrier, inc=1, device_id=peer(here, offset), device_id_type=MESH)
-
+    greeted = [peer(here, offset) for offset in OFFSETS]
+    greeted += [peer(here, tuple((4 - d) % 4 for d in offset), True) for offset in NEAR]
+    greeted.append(twin)
+
+    def greet(devices):
+        for device in devices:
+            pl.semaphore_signal(barrier, inc=1, device_id=device, device_id_type=MESH)
+
+    greet(greeted[:48])
     dims = (((0,), (0,)), ((), ()))
     for i in range(n):
         loads[i].wait()
@@ -87,38 +104,64 @@
         h, l = split(xb[span, :])
         high[span, :] = h
         low[span, :] = l
-        a = lax.dot_general(h, h, dims, preferred_element_type=F32)
+        a0 = lax.dot_general(h[:, :256], h[:, :256], dims, preferred_element_type=F32)
+        a1 = lax.dot_general(h[:, 256:], h, dims, preferred_element_type=F32)
         b = lax.dot_general(h, l, dims, preferred_element_type=F32)
         if i == 0:
-            acc[...] = a
+            acc[:256, :256] = a0
+            acc[256:, :] = a1
             cross[...] = b
+            greet(greeted[48:])
         else:
-            acc[...] += a
+            acc[:256, :256] += a0
+            acc[256:, :] += a1
             cross[...] += b
-    for i in range(4):
-        for j in range(i + 1):
+
+    def fill(blocks):
+        for i, j in blocks:
             si, sj = slice(128 * i, 128 * i + 128), slice(128 * j, 128 * j + 128)
             block = (acc[si, sj] + (cross[si, sj] + cross[sj, si].T)).reshape(8, 2, 8, 128)
             for c in range(2):
                 part[c, block_tiles(i, j)] = block[:, c]
 
-    pl.semaphore_wait(barrier, 1 + len(OFFSETS))
-    swap = pltpu.make_async_remote_copy(
-        src_ref=part.at[1 - core],
-        dst_ref=crecv,
-        send_sem=core_sem.at[0],
-        recv_sem=core_sem.at[1],
-        device_id=twin,
-        device_id_type=MESH,
-    )
-    swap.start()
-    swap.wait()
-    mine[...] = part[core] + crecv[...]
-
-    def second(dz, dx):
-        dy = (12 - s - dz - dx) % 4
+    def swap(tiles, sem):
         return pltpu.make_async_remote_copy(
-            src_ref=mine.at[((z + dz) % 4) * 4 + (x + dx) % 4],
+            src_ref=part.at[1 - core, tiles],
+            dst_ref=crecv.at[tiles],
+            send_sem=sem.at[0],
+            recv_sem=sem.at[1],
+            device_id=twin,
+            device_id_type=MESH,
+        )
+
+    fill([(0, 0), (1, 0), (1, 1), (2, 0)])
+    pl.semaphore_wait(barrier, len(greeted))
+    swap_early, swap_late = swap(pl.ds(0, EARLY), swap_sem), swap(pl.ds(EARLY, 80 - EARLY), swap2_sem)
+    swap_early.start()
+    fill([(2, 1), (2, 2), (3, 0), (3, 1), (3, 2), (3, 3)])
+    swap_late.start()
+    swap_early.wait_recv()
+    mine[:EARLY] = part[core, :EARLY] + crecv[:EARLY]
+    for slot, offset in enumerate(OFFSETS):
+        dz, dx, dy = offset
+        pltpu.make_async_remote_copy(
+            src_ref=mine.at[early_tile((z + dz) % 4, (x + dx) % 4, (s + dz + dx + dy) % 4)],
+            dst_ref=rbuf.at[slot],
+            send_sem=rs_sem.at[0],
+            recv_sem=rs_sem.at[1],
+            device_id=peer(here, offset),
+            device_id_type=MESH,
+        ).start()
+    swap_late.wait_recv()
+    mine[EARLY:] = part[core, EARLY:] + crecv[EARLY:]
+
+    def late_tile(dz, dx, t):
+        return EARLY + 3 * (4 * ((z + dz) % 4) + (x + dx) % 4) + t - 1
+
+    def scatter_late(dz, dx, t):
+        dy = (t + 12 - s - dz - dx) % 4
+        return pltpu.make_async_remote_copy(
+            src_ref=mine.at[late_tile(dz, dx, t)],
             dst_ref=rbuf2.at[16 * dz + 4 * dx + dy],
             send_sem=rs2_sem.at[0],
             recv_sem=rs2_sem.at[1],
@@ -129,102 +172,100 @@
     for dz in (2, 1, 3, 0):
         for dx in (2, 1, 3, 0):
             if (dz, dx) != (0, 0):
-                second(dz, dx).start()
-
-    @pl.when(s != 0)
-    def _():
-        second(0, 0).start()
-
-    for slot, offset in enumerate(OFFSETS):
-        dz, dx, dy = offset
-        pltpu.make_async_remote_copy(
-            src_ref=mine.at[16 + (((z + dz) % 4) * 4 + (x + dx) % 4) * 4 + (y + dy) % 4],
-            dst_ref=rbuf.at[slot],
-            send_sem=rs_sem.at[0],
-            recv_sem=rs_sem.at[1],
-            device_id=peer(here, offset),
-            device_id_type=MESH,
-        ).start()
+                for t in (1, 2, 3):
+                    scatter_late(dz, dx, t).start()
+    for t in (1, 2, 3):
+
+        @pl.when(s != t)
+        def _():
+            scatter_late(0, 0, t).start()
 
     def summed(values):
         while len(values) > 1:
             values = [a + b for a, b in zip(values[0::2], values[1::2])]
         return values[0]
 
-    def gather(tile, sem):
-        for offset in OFFSETS:
-            pltpu.make_async_remote_copy(
-                src_ref=out.at[core, tile],
-                dst_ref=out.at[core, tile],
-                send_sem=sem.at[0],
-                recv_sem=sem.at[1],
-                device_id=peer(here, offset),
-                device_id_type=MESH,
-            ).start()
-
-    def forward(tiles, sem):
-        return pltpu.make_async_remote_copy(
-            src_ref=out.at[core, tiles],
-            dst_ref=out.at[core, tiles],
+    def send_sum(tile, sem, device):
+        pltpu.make_async_remote_copy(
+            src_ref=out.at[core, tile],
+            dst_ref=out.at[core, tile],
             send_sem=sem.at[0],
             recv_sem=sem.at[1],
-            device_id=twin,
+            device_id=device,
             device_id_type=MESH,
-        )
+        ).start()
 
     def settle(ref, sem):
         pltpu.make_async_copy(ref, ref, sem).wait()
 
+    tile = early_tile(z, x, s)
+    settle(rbuf, rs_sem.at[1])
+    terms = {offset: rbuf[slot] for slot, offset in enumerate(OFFSETS)}
+    terms[0, 0, 0] = mine[tile]
+    out[core, tile] = summed([terms[o] + terms[opposite(o)] for o in [(0, 0, 0)] + NEAR])
+    for offset in NEAR:
+        for other in (False, True):
+            send_sum(tile, ag_sem, peer(here, offset, other))
+    send_sum(tile, ag_sem, twin)
+
+    @pl.when(s != 0)
+    def _():
+        late = late_tile(0, 0, s)
+        settle(rbuf2.at[pl.ds(1, 63)], rs2_sem.at[1])
+        out[core, late] = summed([mine[late]] + [rbuf2[slot] for slot in range(1, 64)])
+        for offset in OFFSETS:
+            send_sum(late, ag2_sem, peer(here, offset))
+
+    settle(rbuf, ag_sem.at[1])
+    forward = pltpu.make_async_remote_copy(
+        src_ref=out.at[core, pl.ds(EARLY, 80 - EARLY)],
+        dst_ref=out.at[core, pl.ds(EARLY, 80 - EARLY)],
+        send_sem=fw_sem.at[0],
+        recv_sem=fw_sem.at[1],
+        device_id=twin,
+        device_id_type=MESH,
+    )
+    calls = iter(range(16))
+
+    def between():
+        if next(calls) == FORWARD_AFTER:
+
+            @pl.when(s == 0)
+            def _():
+                settle(rbuf2.at[pl.ds(0, 48)], ag2_sem.at[1])
+
+            @pl.when(s != 0)
+            def _():
+                settle(rbuf2.at[pl.ds(0, 47)], ag2_sem.at[1])
+
+            forward.start()
+
+    block = load_block(out, 0, 0, total) + unit(128)
+    leaf, dets[0] = invert_leaf([block[8 * i : 8 * i + 8] for i in range(16)], between)
+    leaf = jnp.concatenate(leaf, axis=0)
+    inverse0[...] = leaf
+    side = load_block(out, 1, 0, total)
+    first = dot_exact(leaf, side.T)
+    first0[...] = first
+    block = load_block(out, 1, 1, total) + unit(128) - dot_exact(side, first)
+    leaf, dets[1] = invert_leaf([block[8 * i : 8 * i + 8] for i in range(16)], between)
+    inverse1[...] = jnp.concatenate(leaf, axis=0)
+
+    swap_early.wait_send()
+    swap_late.wait_send()
+    settle(rbuf, rs_sem.at[0])
+    settle(rbuf, ag_sem.at[0])
+
     @pl.when(s == 0)
     def _():
-        settle(rbuf2.at[pl.ds(1, 63)], rs2_sem.at[1])
-        out[core, 4 * z + x] = summed([mine[4 * z + x]] + [rbuf2[slot] for slot in range(1, 64)])
-        gather(4 * z + x, ag2_sem)
-
-    chip = (z * 4 + x) * 4 + y
-    settle(rbuf, rs_sem.at[1])
-    out[core, 16 + chip] = summed([mine[16 + chip]] + [rbuf[slot] for slot in range(63)])
-    gather(16 + chip, ag_sem)
-
-    @pl.when(s == 0)
-    def _():
-        settle(rbuf2.at[pl.ds(0, 15)], ag2_sem.at[1])
+        settle(rbuf2.at[pl.ds(0, 48)], rs2_sem.at[0])
 
     @pl.when(s != 0)
     def _():
-        settle(rbuf2.at[pl.ds(0, 16)], ag2_sem.at[1])
-
-    ahead = forward(pl.ds(0, 16), fw2_sem)
-    ahead.start()
-    ahead.wait_recv()
-    later = forward(pl.ds(16, 64), fw_sem)
-    calls = iter(range(8))
-
-    def between():
-        if next(calls) == FORWARD_AFTER:
-            settle(rbuf, ag_sem.at[1])
-            later.start()
-
-    block = load_block(out, 0, 0, total) + unit(128)
-    leaf, dets[...] = invert_leaf([block[8 * i : 8 * i + 8] for i in range(16)], between)
-    leaf = jnp.concatenate(leaf, axis=0)
-    inverse[...] = leaf
-    first[...] = dot_exact(leaf, load_block(out, 1, 0, total).T)
-
-    settle(rbuf, rs_sem.at[0])
-    settle(rbuf, ag_sem.at[0])
-
-    @pl.when(s == 0)
-    def _():
-        settle(rbuf2.at[pl.ds(0, 15)], rs2_sem.at[0])
+        settle(rbuf2.at[pl.ds(0, 47)], rs2_sem.at[0])
         settle(rbuf, ag2_sem.at[0])
 
-    @pl.when(s != 0)
-    def _():
-        settle(rbuf2.at[pl.ds(0, 16)], rs2_sem.at[0])
-
-    ahead.wait_send()
-    later.wait()
+    forward.wait()
 
 
 def sub_row(x, s):
@@ -306,7 +347,7 @@
     return jnp.dot(ah, bh, preferred_element_type=F32) + small
 
 
-def map_kernel(total, gram, high, low, inverse0, first0, dets0, out_hbm, logdet, ob, zh, zl, mat, store_sem):
+def map_kernel(total, gram, high, low, inverse0, first0, inverse1, dets0, out_hbm, logdet, ob, zh, zl, mat, store_sem):
     rows, k = high.shape
     n = rows // CHUNK
     for i in range(k // 128):
@@ -333,22 +374,25 @@
         ob[span, :half] = d[:, :half]
         zh[span, :], zl[span, :] = split((high[span, half:].astype(F32) + low[span, half:].astype(F32)) - d[:, half:])
 
-    logs = jnp.log(dets0[...])
+    logs = jnp.log(dets0[0]) + jnp.log(dets0[1])
     for b in range(count):
         lo, hi = 128 * b, 128 * (b + 1)
         base = 0 if lo < half else half
         if b == 0:
             inverse = inverse0[...]
+        elif b == 1:
+            inverse = inverse1[...]
         else:
             leaf, dets = invert_leaf(
-                [block[8 * i : 8 * i + 8] for i in range(16)], forward_chunk if base else lambda: None
+                [block[8 * i : 8 * i + 8] for i in range(16)], forward_chunk
             )
             logs = logs + jnp.log(dets)
             inverse = jnp.concatenate(leaf, axis=0)
         sides = {i: mat[128 * i : 128 * i + 128, lo:hi] for i in range(base // 128, count)}
         if b + 1 < count:
             first = dot_exact(inverse, mat[lo:hi, hi : hi + 128]) if b else first0[...]
-            block = mat[hi : hi + 128, hi : hi + 128] - dot_exact(sides[b + 1], first)
+            if b:
+                block = mat[hi : hi + 128, hi : hi + 128] - dot_exact(sides[b + 1], first)
         parts = []
         if lo > base:
             parts.append(dot_exact(inverse, mat[lo:hi, base:lo]))
@@ -402,10 +446,11 @@
             jax.ShapeDtypeStruct((rows, k), BF16),
             jax.ShapeDtypeStruct((128, 128), F32),
             jax.ShapeDtypeStruct((128, 128), F32),
-            jax.ShapeDtypeStruct((8, 128), F32),
+            jax.ShapeDtypeStruct((128, 128), F32),
+            jax.ShapeDtypeStruct((2, 8, 128), F32),
         ),
         in_specs=[HBM],
-        out_specs=(VMEM,) * 6,
+        out_specs=(VMEM,) * 7,
         scratch_shapes=[
             pltpu.VMEM((rows, k), F32),
             pltpu.VMEM((k, k), F32),
@@ -424,12 +469,12 @@
     )(pltpu.with_memory_space_constraint(sketch, pltpu.HBM))
 
 
-def invert_and_map(total, gram, high, low, inverse, first, dets):
+def invert_and_map(total, gram, high, low, inverse0, first0, inverse1, dets):
     rows, k = high.shape
     return pl.pallas_call(
         functools.partial(map_kernel, total),
         out_shape=(jax.ShapeDtypeStruct((rows, k), F32), jax.ShapeDtypeStruct((1, 1), F32)),
-        in_specs=[VMEM] * 6,
+        in_specs=[VMEM] * 7,
         out_specs=(HBM, pl.BlockSpec(memory_space=pltpu.SMEM)),
         scratch_shapes=[
             pltpu.VMEM((rows, k), F32),
@@ -440,7 +485,7 @@
         ],
         compiler_params=pltpu.CompilerParams(vmem_limit_bytes=VMEM_LIMIT),
         name="invert_and_map",
-    )(gram, high, low, inverse, first, dets)
+    )(gram, high, low, inverse0, first0, inverse1, dets)
 
 
 def on_device(sketch):

time: 51.2 us -> 49.2 us (0.961)
  Pallas kernels: 50.2 us -> 48.3 us
    pallas_call x1, Pallas kernels: 17.8 us -> 15.4 us  [invert_and_map(): pl.pallas_call(functools.partial(map_kernel, total), out_shape=(jax.Shape...]
    pallas_call x1, Pallas kernels: 32.4 us -> 32.9 us  [gram_sum(): pl.pallas_call(functools.partial(gram_kernel, total), out_shape=(jax.Shap...]
where the time goes in v4:
time: 49.2 us; the launch traced here: 49.1 us
  Pallas kernels  48.3 us (98%)
  between operations  0.82 us (2%)
    pallas_call x1, Pallas kernels, gram_sum(): pl.pallas_call(functools.partial(gram_kernel, total), out_shape=(jax.Shap...  32.9 us
    pallas_call x1, Pallas kernels, invert_and_map(): pl.pallas_call(functools.partial(map_kernel, total), out_shape=(jax.Shape...  15.4 us

profile of v4, /device:TPU:1, one launch (start us, length us, event | category | flops | bytes accessed | tf_op | source)
XLA Modules:
  0.0 49.1 jit_solution(17081799591157326923)
XLA Ops:
  0.6 32.9 %gram_sum.1 = (f32[2,80,8,128]{3,2,1,0:T(8,128)S(1)}, bf16[4096,512]{1,0:T(8,128)(2,1)S(1)}, bf16[4096,512]{1,0:T(8,128)(2,1)S(1)}, f32[128,128]{1,0:T(8,128)S(1...) custom-call(f32[4096,512]{1,0:T(8,128)} %x_hbm.1), custom_call_target="tpu_custom_call" | custom-call | tf_op jit(solution)/shard_map/gram_sum/pallas_call | solution.py:441
  33.6 15.4 %invert_and_map.1 = (f32[4096,512]{1,0:T(8,128)}, f32[1,1]{1,0:T(1,128)}) custom-call(f32[2,80,8,128]{3,2,1,0:T(8,128)S(1)} %get-tuple-element.11.gram, bf16[4096,512]{1,0:T(8,128)(2,1)S(1)} %get-tuple-element.12.high, bf16[4096,512]{1,0:T(8,128)(2,1)S(1)} %get-tuple-element.13.low, f32[128,128]{1,0:T(8,128)S(1)} %get-tuple-element.14.inverse0, ...), custom_call_target="tpu_custom_call" | custom-call | tf_op jit(solution)/shard_map/invert_and_map/pallas_call | solution.py:474

commit v5 on v4

--- a/solution.py
+++ b/solution.py
@@ -12,7 +12,7 @@
 VMEM_LIMIT = 36 * 2**20
 CHUNK = 512
 STORE = 256
-GROUP = 16
+FORWARD = 256
 FORWARD_AFTER = 6
 
 
@@ -70,7 +70,7 @@
 
 
 def gram_kernel(
-    total, x_hbm, out, high, low, inverse0, first0, inverse1, dets, xb, acc, cross, part, crecv, mine, recv,
+    total, x_hbm, out, high, low, inverse0, first0, third0, inverse1, dets, xb, acc, cross, part, crecv, mine, recv,
     load_sem, swap_sem, swap2_sem, rs_sem, rs2_sem, ag_sem, ag2_sem, fw_sem,
 ):
     rows = x_hbm.shape[0]
@@ -180,11 +180,6 @@
         def _():
             scatter_late(0, 0, t).start()
 
-    def summed(values):
-        while len(values) > 1:
-            values = [a + b for a, b in zip(values[0::2], values[1::2])]
-        return values[0]
-
     def send_sum(tile, sem, device):
         pltpu.make_async_remote_copy(
             src_ref=out.at[core, tile],
@@ -202,7 +197,7 @@
     settle(rbuf, rs_sem.at[1])
     terms = {offset: rbuf[slot] for slot, offset in enumerate(OFFSETS)}
     terms[0, 0, 0] = mine[tile]
-    out[core, tile] = summed([terms[o] + terms[opposite(o)] for o in [(0, 0, 0)] + NEAR])
+    out[core, tile] = tree_sum([terms[o] + terms[opposite(o)] for o in [(0, 0, 0)] + NEAR])
     for offset in NEAR:
         for other in (False, True):
             send_sum(tile, ag_sem, peer(here, offset, other))
@@ -212,7 +207,7 @@
     def _():
         late = late_tile(0, 0, s)
         settle(rbuf2.at[pl.ds(1, 63)], rs2_sem.at[1])
-        out[core, late] = summed([mine[late]] + [rbuf2[slot] for slot in range(1, 64)])
+        out[core, late] = tree_sum([mine[late]] + [rbuf2[slot] for slot in range(1, 64)])
         for offset in OFFSETS:
             send_sum(late, ag2_sem, peer(here, offset))
 
@@ -247,6 +242,7 @@
     side = load_block(out, 1, 0, total)
     first = dot_exact(leaf, side.T)
     first0[...] = first
+    third0[...] = dot_exact(leaf, load_block(out, 2, 0, total).T)
     block = load_block(out, 1, 1, total) + unit(128) - dot_exact(side, first)
     leaf, dets[1] = invert_leaf([block[8 * i : 8 * i + 8] for i in range(16)], between)
     inverse1[...] = jnp.concatenate(leaf, axis=0)
@@ -266,6 +262,12 @@
         settle(rbuf, ag2_sem.at[0])
 
     forward.wait()
+
+
+def tree_sum(values):
+    while len(values) > 1:
+        values = [a + b for a, b in zip(values[0::2], values[1::2])]
+    return values[0]
 
 
 def sub_row(x, s):
@@ -281,53 +283,61 @@
     sub = lax.broadcasted_iota(jnp.int32, (8, 128), 0)
     rows = list(rows)
     dets = jnp.ones((8, 128), F32)
-    zero = jnp.zeros((8, 128), F32)
-    nv = GROUP // 8
-    for g in range(128 // GROUP):
-        a = GROUP * g
-        own = [nv * g + v for v in range(nv)]
-        near = [i for i in range(own[-1] + 1, own[-1] + 1 + nv) if i < 16]
-        cols = [[lane_col(rows[m], a + j) for m in own] for j in range(GROUP)]
-        left = {i: [lane_col(rows[i], a + j) for j in range(GROUP)] for i in near}
-        inside = (lane >= a) & (lane < a + GROUP)
-        top = [jnp.where(inside, (lane - a == sub + 8 * v).astype(F32), rows[m]) for v, m in enumerate(own)]
-        diag, off = [zero] * nv, [zero] * nv
-        for k in range(0, GROUP, 2):
-            v0, s0 = divmod(k, 8)
+
+    def eliminate(a, cols, top, dets):
+        nv = len(top)
+        diag = off = jnp.zeros((8, 128), F32)
+        for k in range(0, 8, 2):
             c0, c1 = cols[k], cols[k + 1]
-            p00, p10 = sub_row(c0[v0], s0), sub_row(c0[v0], s0 + 1)
-            p01, p11 = sub_row(c1[v0], s0), sub_row(c1[v0], s0 + 1)
+            p00, p10 = sub_row(c0[0], k), sub_row(c0[0], k + 1)
+            p01, p11 = sub_row(c1[0], k), sub_row(c1[0], k + 1)
             det = p00 * p11 - p01 * p10
             r = 1.0 / det
             dets = jnp.where(lane == a + k, det, dets)
-            diag[v0] = jnp.where(sub == s0, p11 * r, jnp.where(sub == s0 + 1, p00 * r, diag[v0]))
-            off[v0] = jnp.where(sub == s0, -p01 * r, jnp.where(sub == s0 + 1, -p10 * r, off[v0]))
+            diag = jnp.where(sub == k, p11 * r, jnp.where(sub == k + 1, p00 * r, diag))
+            off = jnp.where(sub == k, -p01 * r, jnp.where(sub == k + 1, -p10 * r, off))
+            pair = (sub == k) | (sub == k + 1)
             n0 = [c0[v] * p11 - c1[v] * p10 for v in range(nv)]
             n1 = [c1[v] * p00 - c0[v] * p01 for v in range(nv)]
-            pair = (sub == s0) | (sub == s0 + 1)
-            n0[v0] = jnp.where(pair, 0.0, n0[v0])
-            n1[v0] = jnp.where(pair, 0.0, n1[v0])
+            n0[0], n1[0] = jnp.where(pair, 0.0, n0[0]), jnp.where(pair, 0.0, n1[0])
             f0, f1 = [n * r for n in n0], [n * r for n in n1]
-            for j in range(k + 2, GROUP):
-                b0, b1 = sub_row(cols[j][v0], s0), sub_row(cols[j][v0], s0 + 1)
-                if j < k + 4:
-                    cols[j] = [cols[j][v] - (n0[v] * b0 + n1[v] * b1) * r for v in range(nv)]
+            for j in range(k + 2, len(cols)):
+                if j < 8:
+                    b0, b1 = sub_row(cols[j][0], k), sub_row(cols[j][0], k + 1)
                 else:
-                    cols[j] = [cols[j][v] - (f0[v] * b0 + f1[v] * b1) for v in range(nv)]
-            b0, b1 = sub_row(top[v0], s0), sub_row(top[v0], s0 + 1)
+                    b0, b1 = sub_row(c0[1], j - 8), sub_row(c1[1], j - 8)
+                for v in range(nv) if j < 8 else range(1, nv):
+                    if j < k + 4:
+                        cols[j][v] = cols[j][v] - (n0[v] * b0 + n1[v] * b1) * r
+                    else:
+                        cols[j][v] = cols[j][v] - (f0[v] * b0 + f1[v] * b1)
+            b0, b1 = sub_row(top[0], k), sub_row(top[0], k + 1)
             top = [top[v] - (f0[v] * b0 + f1[v] * b1) for v in range(nv)]
-        swapped = [jnp.where(sub % 2 == 0, pltpu.roll(t, 7, 0), pltpu.roll(t, 1, 0)) for t in top]
-        top = [diag[v] * top[v] + off[v] * swapped[v] for v in range(nv)]
-        spread = [sub_row(top[j // 8], j % 8) for j in range(GROUP)]
-        new = dict(zip(own, top))
+        swapped = jnp.where(sub % 2 == 0, pltpu.roll(top[0], 7, 0), pltpu.roll(top[0], 1, 0))
+        return [diag * top[0] + off * swapped] + top[1:], dets
+
+    for g in range(8):
+        a = 16 * g
+        near = [2 * g + 2, 2 * g + 3] if g < 7 else []
+        cols = [[lane_col(rows[2 * g + v], a + j) for v in range(2)] for j in range(8)]
+        cols += [[None, lane_col(rows[2 * g + 1], a + 8 + j)] for j in range(8)]
+        left = {i: [lane_col(rows[i], a + j) for j in range(16)] for i in near}
+        inside, half0, half1 = (lane >= a) & (lane < a + 16), (lane >= a) & (lane < a + 8), (lane >= a + 8) & (lane < a + 16)
+        top = [jnp.where(half0, (lane - a == sub).astype(F32), rows[2 * g]), jnp.where(half0, 0.0, rows[2 * g + 1])]
+        (top0, top1), dets = eliminate(a, cols, top, dets)
+        cross = [lane_col(top0, a + 8 + j) for j in range(8)]
+        top1 = jnp.where(half1, (lane - a - 8 == sub).astype(F32), top1)
+        (top1,), dets = eliminate(a + 8, [[c[1]] for c in cols[8:]], [top1], dets)
+        spread = [sub_row(top1, j) for j in range(8)]
+        terms = [cross[j] * spread[j] for j in range(8)]
+        top0 = jnp.where(half1, 0.0, top0) - tree_sum(terms)
+        spread = [sub_row(top0, j) for j in range(8)] + spread
+        new = {2 * g: top0, 2 * g + 1: top1}
         for i in near:
-            terms = [left[i][j] * spread[j] for j in range(GROUP)]
-            while len(terms) > 1:
-                terms = [s + t for s, t in zip(terms[0::2], terms[1::2])]
-            new[i] = jnp.where(inside, 0.0, rows[i]) - terms[0]
-        padded = [jnp.zeros((a, 128), F32)] * (a > 0) + top + [jnp.zeros((128 - a - GROUP, 128), F32)] * (a + GROUP < 128)
+            new[i] = jnp.where(inside, 0.0, rows[i]) - tree_sum([left[i][j] * spread[j] for j in range(16)])
+        padded = [jnp.zeros((a, 128), F32)] * (a > 0) + [top0, top1] + [jnp.zeros((112 - a, 128), F32)] * (a < 112)
         padded = jnp.concatenate(padded, axis=0)
-        for start, stop in ((0, own[0]), (own[-1] + 1 + len(near), 16)):
+        for start, stop in ((0, 2 * g), (2 * g + 2 + len(near), 16)):
             if stop > start:
                 update = dot_exact(jnp.concatenate(rows[start:stop], axis=0), padded)
                 for i in range(start, stop):
@@ -343,13 +353,13 @@
 
 def dot3(a, b):
     (ah, al), (bh, bl) = a, b
-    small = jnp.dot(al, bh, preferred_element_type=F32) + jnp.dot(ah, bl, preferred_element_type=F32)
-    return jnp.dot(ah, bh, preferred_element_type=F32) + small
-
-
-def map_kernel(total, gram, high, low, inverse0, first0, inverse1, dets0, out_hbm, logdet, ob, zh, zl, mat, store_sem):
+    return jnp.dot(
+        jnp.concatenate([ah, al, ah], axis=1), jnp.concatenate([bh, bh, bl], axis=0), preferred_element_type=F32
+    )
+
+
+def map_kernel(total, gram, high, low, inverse0, first0, third0, inverse1, dets0, out_hbm, logdet, ob, zh, zl, mat, store_sem):
     rows, k = high.shape
-    n = rows // CHUNK
     for i in range(k // 128):
         for j in range(i + 1):
             block = load_block(gram, i, j, total)
@@ -360,7 +370,7 @@
             mat[128 * i : 128 * i + 128, 128 * j : 128 * j + 128] = block
 
     half, count = k // 2, k // 128
-    early = iter(range(n))
+    early = iter(range(rows // FORWARD))
     weights = []
 
     def forward_chunk():
@@ -369,7 +379,7 @@
             return
         if not weights:
             weights.extend(split(mat[:half, :]))
-        span = slice(i * CHUNK, (i + 1) * CHUNK)
+        span = slice(i * FORWARD, (i + 1) * FORWARD)
         d = dot3((high[span, :half], low[span, :half]), weights)
         ob[span, :half] = d[:, :half]
         zh[span, :], zl[span, :] = split((high[span, half:].astype(F32) + low[span, half:].astype(F32)) - d[:, half:])
@@ -399,8 +409,12 @@
         parts.append(inverse)
         if b + 1 < count:
             parts.append(first)
-        if hi + 128 < k:
-            parts.append(dot_exact(inverse, mat[lo:hi, hi + 128 :]))
+        after = hi + 128
+        if b == 0:
+            parts.append(third0[...])
+            after += 128
+        if after < k:
+            parts.append(dot_exact(inverse, mat[lo:hi, after:]))
         top = jnp.concatenate(parts, axis=1)
         for i in sides:
             if i != b:
@@ -447,10 +461,11 @@
             jax.ShapeDtypeStruct((128, 128), F32),
             jax.ShapeDtypeStruct((128, 128), F32),
             jax.ShapeDtypeStruct((128, 128), F32),
+            jax.ShapeDtypeStruct((128, 128), F32),
             jax.ShapeDtypeStruct((2, 8, 128), F32),
         ),
         in_specs=[HBM],
-        out_specs=(VMEM,) * 7,
+        out_specs=(VMEM,) * 8,
         scratch_shapes=[
             pltpu.VMEM((rows, k), F32),
             pltpu.VMEM((k, k), F32),
@@ -469,12 +484,12 @@
     )(pltpu.with_memory_space_constraint(sketch, pltpu.HBM))
 
 
-def invert_and_map(total, gram, high, low, inverse0, first0, inverse1, dets):
+def invert_and_map(total, gram, high, low, inverse0, first0, third0, inverse1, dets):
     rows, k = high.shape
     return pl.pallas_call(
         functools.partial(map_kernel, total),
         out_shape=(jax.ShapeDtypeStruct((rows, k), F32), jax.ShapeDtypeStruct((1, 1), F32)),
-        in_specs=[VMEM] * 7,
+        in_specs=[VMEM] * 8,
         out_specs=(HBM, pl.BlockSpec(memory_space=pltpu.SMEM)),
         scratch_shapes=[
             pltpu.VMEM((rows, k), F32),
@@ -485,7 +500,7 @@
         ],
         compiler_params=pltpu.CompilerParams(vmem_limit_bytes=VMEM_LIMIT),
         name="invert_and_map",
-    )(gram, high, low, inverse0, first0, inverse1, dets)
+    )(gram, high, low, inverse0, first0, third0, inverse1, dets)
 
 
 def on_device(sketch):

time: 49.2 us -> 48 us (0.976)
  Pallas kernels: 48.3 us -> 47 us
    pallas_call x1, Pallas kernels: 15.4 us -> 14.2 us  [invert_and_map(): pl.pallas_call(functools.partial(map_kernel, total), out_shape=(jax.Shape...]
where the time goes in v5:
time: 48 us; the launch traced here: 47.9 us
  Pallas kernels  47 us (98%)
  between operations  0.82 us (2%)
    pallas_call x1, Pallas kernels, gram_sum(): pl.pallas_call(functools.partial(gram_kernel, total), out_shape=(jax.Shap...  32.8 us
    pallas_call x1, Pallas kernels, invert_and_map(): pl.pallas_call(functools.partial(map_kernel, total), out_shape=(jax.Shape...  14.2 us

profile of v5, /device:TPU:1, one launch (start us, length us, event | category | flops | bytes accessed | tf_op | source)
XLA Modules:
  0.0 47.9 jit_solution(13692945887350899194)
XLA Ops:
  0.6 32.8 %gram_sum.1 = (f32[2,80,8,128]{3,2,1,0:T(8,128)S(1)}, bf16[4096,512]{1,0:T(8,128)(2,1)S(1)}, bf16[4096,512]{1,0:T(8,128)(2,1)S(1)}, f32[128,128]{1,0:T(8,128)S(1...) custom-call(f32[4096,512]{1,0:T(8,128)} %x_hbm.1), custom_call_target="tpu_custom_call" | custom-call | tf_op jit(solution)/shard_map/gram_sum/pallas_call | solution.py:455
  33.5 14.2 %invert_and_map.1 = (f32[4096,512]{1,0:T(8,128)}, f32[1,1]{1,0:T(1,128)}) custom-call(f32[2,80,8,128]{3,2,1,0:T(8,128)S(1)} %get-tuple-element.12.gram, bf16[4096,512]{1,0:T(8,128)(2,1)S(1)} %get-tuple-element.13.high, bf16[4096,512]{1,0:T(8,128)(2,1)S(1)} %get-tuple-element.14.low, f32[128,128]{1,0:T(8,128)S(1)} %get-tuple-element.15.inverse0, ...), custom_call_target="tpu_custom_call" | custom-call | tf_op jit(solution)/shard_map/invert_and_map/pallas_call | solution.py:489
